TPU v7x, 256 devices: a whole 4x4x8 slice. The times are simulated.
256 devices in a mesh: dp: 16 (over x, y), tensor: 16 (over z, core).
Axes of the slice: x: 4, y: 4, z: 8, core: 2. Of those that a mesh axis runs over, the one named last changes fastest.
Arguments:
- activations: bfloat16 [32, 1024, 28672], P('dp', None, 'tensor'), may hold values from -6 to 6
- out_grads: bfloat16 [32, 1024, 8192], P('dp', None, 'tensor'), may hold values from -6 to 6
- in_factor: bfloat16 [64, 28672], P(None, 'tensor'), may hold values from -0.03125 to 0.03125
- out_factor: bfloat16 [64, 8192], P(None, 'tensor'), may hold values from -0.001953125 to 0.001953125
- queries: bfloat16 [1024, 4096], P('dp', 'tensor'), may hold values from -0.125 to 0.125
Outputs:
- projected_grads: bfloat16 [32, 4096], P('dp', 'tensor')
- scores: float32 [32, 1024], P('dp', 'tensor')
All inputs are finite; a program needn't handle non-finite values.
Results may differ from a plain program's by a relative error of at most 0.0057.
Values may be sent and summed in bfloat16 or wider, within the bound.
No kernel may reach another device: no remote copies, remote signals or barrier semaphores. Data moves between devices by JAX's collectives and lax.ppermute only.
A program may use at most 64 MiB of HBM per device.

v0:
```python
import jax
import jax.numpy as jnp
from jax import lax
from jax.sharding import PartitionSpec as P

RANK = 64


def local(activations, out_grads, in_factor, out_factor, queries):
    tensor_size = lax.axis_size("tensor")
    slice_width = RANK // tensor_size
    input_part = jnp.einsum(
        "esf,rf->esr", activations, in_factor, preferred_element_type=jnp.float32
    )
    grad_part = jnp.einsum("esd,rd->esr", out_grads, out_factor, preferred_element_type=jnp.float32)
    paired = jnp.concatenate([input_part, grad_part], axis=2)
    example_count = paired.shape[0]
    summed = lax.psum(paired, "tensor").astype(jnp.bfloat16)
    own_rows = lax.dynamic_slice_in_dim(
        summed[:, :, :RANK], lax.axis_index("tensor") * slice_width, slice_width, 2
    )
    product = jnp.einsum(
        "esi,esj->eij", own_rows, summed[:, :, RANK:], preferred_element_type=jnp.float32
    )
    gradients = product.reshape(example_count, slice_width * RANK).astype(jnp.bfloat16)
    partial_value = jnp.einsum(
        "eg,qg->eq",
        gradients,
        lax.all_gather(queries, "dp", axis=0, tiled=True),
        preferred_element_type=jnp.float32,
    )
    scores = lax.psum_scatter(partial_value, "tensor", scatter_dimension=1, tiled=True)
    return (gradients, scores)


def solution(mesh):
    placed = (
        P("dp", None, "tensor"),
        P("dp", None, "tensor"),
        P(None, "tensor"),
        P(None, "tensor"),
        P("dp", "tensor"),
    )
    return jax.shard_map(
        local,
        mesh=mesh,
        in_specs=placed,
        out_specs=(P("dp", "tensor"), P("dp", "tensor")),
        check_vma=False,
    )
```

profile of v0, /device:TPU:1, one launch (start us, length us, event | category | flops | bytes accessed | tf_op | source)
XLA Modules:
  0.0 164.4 jit_solution(12277233084746343226)
XLA Ops:
  7.2 0.0 copy-start
  7.2 0.0 reduce-scatter.4.cloned.1.call-start
  7.2 1.5 copy-done
  8.8 0.0 copy-start.1
  8.8 1.6 fusion.3
  10.4 5.4 %fusion.1 = f32[2,1024,64]{1,2,0:T(8,128)S(1)} fusion(bf16[2,1024,1792]{2,1,0:T(8,128)(2,1)} %param.5, bf16[64,1792]{1,0:T(8,128)(2,1)} %param.7), kind=kOutput, calls=%fused_computation.4 | convolution fusion | flops 469762048 | bytes 8093696 | tf_op jit(solution)/shard_map/esf,rf->esr/dot_general | solution.py:12
  15.8 0.1 pad_maximum_fusion
  15.8 60.1 %all-reduce.1 = bf16[2,1024,128]{1,2,0:T(8,128)(2,1)} all-reduce(f32[2,1024,128]{1,2,0:T(8,128)S(1)} %pad_maximum_fusion), channel_id=1, replica_groups=mesh['dp'=16,'tensor'=16] {'tensor'}, use_global_device_ids=true, to_apply=%region_0.0 | all-reduce | flops 262144 | bytes 1572864 | tf_op jit(solution)/shard_map/psum | solution.py:18
  76.0 1.0 slice.8
  76.9 1.1 convolution_convert_fusion
  78.1 0.1 convert_element_type.11
  78.2 0.0 copy-done.1
  78.2 0.0 copy-start.2
  78.2 19.1 %all_gather.3 = bf16[1024,256]{1,0:T(8,128)(2,1)S(1)} all-gather(bf16[64,256]{1,0:T(8,128)(2,1)S(1)} %copy-done.1), channel_id=1, replica_groups=mesh['dp'=16,'tensor'=16] {'dp'}, dimensions={0}, use_global_device_ids=true | all-gather | bytes 557056 | tf_op jit(solution)/shard_map/all_gather | solution.py:29
  97.2 1.0 convolution_bitcast_fusion
  98.3 0.0 reduce-scatter.4.cloned.1.call-update
  98.3 57.8 %reduce-scatter.4.cloned.1.call-done = f32[64,2]{1,0:T(8,128)} async-done(((f32[1024,2]{1,0:T(8,128)}), f32[64,2]{1,0:T(8,128)}) %reduce-scatter.4.cloned.1.call-update) | async-done | bytes 528
  156.1 1.4 copy.8
  157.5 0.0 copy-done.2
Async XLA Ops:
  7.2 1.6 copy-start
  7.2 148.9 %reduce-scatter.4.cloned.1.call-start = ((), (), s32[]{:S(2)}) async-start(), calls=%async_computation.1 | async-start | bytes 557056
  8.8 69.4 %copy-start.1 = (bf16[64,256]{1,0:T(8,128)(2,1)S(1)}, bf16[64,256]{1,0:T(8,128)(2,1)}, u32[]{:S(2)}) copy-start(bf16[64,256]{1,0:T(8,128)(2,1)} %param.9) | copy-start | bytes 98308
  78.2 79.4 %copy-start.2 = (bf16[2,256]{1,0:T(2,128)(2,1)}, bf16[2,256]{1,0:T(2,128)(2,1)S(1)}, u32[]{:S(2)}) copy-start(bf16[2,256]{1,0:T(2,128)(2,1)S(1)} %convert_element_type.11) | copy-start | bytes 3076
Sparse Core Ops, SparseCore 0:
  98.4 57.6 reduce-scatter.3
where the time goes:
time: 167 us; the launch traced here: 164 us
  blocking collectives  79.2 us (47%)
  waiting for transfers between devices  57.8 us (35%)
  between operations  14.1 us (8%)
  matrix products  9.16 us (5%)
  local copies, waits for them, and re-layouts  3.99 us (2%)
    psum x1, blocking collectives, local(): summed = lax.psum(paired, 'tensor').astype(jnp.bfloat16)  60.1 us
    unnamed x2, waiting for transfers between devices  57.8 us
    all_gather x1, blocking collectives, local(): lax.all_gather(queries, 'dp', axis=0, tiled=True)  19.1 us
    dot_general x1, matrix products, local(): jnp.einsum('esf,rf->esr', activations, in_factor, preferred_element_type=...  5.4 us
  transfers between devices with their start and end apart: 1, of which 1 were waited for; matrix products, arithmetic and copies ran while one was open for 0% of the time, Pallas kernels for 0%

commit v1 on v0

v1 whole, which is shorter than its diff:
```python
import jax
import jax.numpy as jnp
import numpy as np
from jax import lax
from jax.experimental import pallas as pl
from jax.experimental.pallas import tpu as pltpu
from jax.sharding import PartitionSpec as P

RANK = 64
LANES = 128
F32 = jnp.float32
BF16 = jnp.bfloat16
MIB = 1024 * 1024
NT = (((1,), (1,)), ((), ()))
TN = (((0,), (0,)), ((), ()))
SMEM = pl.BlockSpec(memory_space=pltpu.SMEM)
VMEM = pl.BlockSpec(memory_space=pltpu.VMEM)
ANY = pl.BlockSpec(memory_space=pl.ANY)


def shaped(shape, dtype):
    return jax.ShapeDtypeStruct(shape, dtype)


def project_kernel(which, acts, grads, inf, outf, out):
    del which
    left = lax.dot_general(acts[0], inf[...], NT, preferred_element_type=F32)
    right = lax.dot_general(grads[0], outf[...], NT, preferred_element_type=F32)
    out[...] = jnp.concatenate([left, right], axis=1)


def project(which, acts, grads, inf, outf):
    _, seq, ff = acts.shape
    d = grads.shape[2]
    rows = seq // 2
    held = [pltpu.with_memory_space_constraint(x, pltpu.HBM) for x in (acts, grads, inf, outf)]
    return pl.pallas_call(
        project_kernel,
        out_shape=pltpu.VMEM((seq, 2 * RANK), F32),
        grid_spec=pltpu.PrefetchScalarGridSpec(
            num_scalar_prefetch=1,
            grid=(seq // rows,),
            in_specs=[
                pl.BlockSpec((1, rows, ff), lambda i, w: (w[0], i, 0)),
                pl.BlockSpec((1, rows, d), lambda i, w: (w[0], i, 0)),
                pl.BlockSpec((RANK, ff), lambda i, w: (0, 0)),
                pl.BlockSpec((RANK, d), lambda i, w: (0, 0)),
            ],
            out_specs=pl.BlockSpec((rows, 2 * RANK), lambda i, w: (i, 0)),
        ),
        compiler_params=pltpu.CompilerParams(vmem_limit_bytes=24 * MIB),
        cost_estimate=pl.CostEstimate(
            flops=2 * seq * (ff + d) * RANK,
            bytes_accessed=2 * seq * (ff + d),
            transcendentals=0,
        ),
        name="project",
    )(which, *held)


def pair_kernel(kept, arrived, block, out, same):
    out[...] = (kept[...] + arrived[...]).astype(BF16)
    same[...] = block[...]


def pair_sum(kept, arrived, block):
    return pl.pallas_call(
        pair_kernel,
        out_shape=(shaped(kept.shape, BF16), shaped(block.shape, BF16)),
        in_specs=[VMEM] * 3,
        out_specs=(VMEM, VMEM),
        compiler_params=pltpu.CompilerParams(vmem_limit_bytes=8 * MIB),
        name="pair_sum",
    )(kept, arrived, block)


def product_kernel(parts, *refs):
    blocks = refs[:-3]
    out, joined, square = refs[-3:]
    total = jnp.sum(parts[...].astype(F32), axis=0)
    square[...] = lax.dot_general(
        total[:, :RANK],
        total[:, RANK:],
        TN,
        precision=lax.Precision.HIGHEST,
        preferred_element_type=F32,
    )
    half = RANK // 2
    rows = jnp.concatenate(
        [square[pl.ds(0, half, stride=2), :], square[pl.ds(1, half, stride=2), :]], axis=1
    )
    for copy in range(out.shape[0]):
        out[copy] = rows
    for n, block in enumerate(blocks):
        joined[n] = block[...]


def product(parts, copies, blocks):
    return pl.pallas_call(
        product_kernel,
        out_shape=(
            shaped((copies, RANK * RANK // LANES, LANES), F32),
            shaped((len(blocks),) + blocks[0].shape, BF16),
        ),
        in_specs=[VMEM] * (1 + len(blocks)),
        out_specs=(VMEM, VMEM),
        scratch_shapes=[pltpu.VMEM((RANK, RANK), F32)],
        compiler_params=pltpu.CompilerParams(vmem_limit_bytes=8 * MIB),
        name="product",
    )(parts, *blocks)


def finish_kernel(place, parts, *refs):
    pieces = refs[:-3]
    gradients, scores, held = refs[-3:]
    tensor = place[0]
    devices, rows, _ = parts.shape
    for example in range(2):
        total = parts[example]
        for z in range(1, devices // 2):
            total = total + parts[2 * z + example]
        held[example * rows : (example + 1) * rows] = total.astype(BF16).astype(F32)
    blocks = rows // devices
    mine = [
        jnp.concatenate(
            [held[pl.ds(e * rows + tensor * blocks + b, 1), :] for b in range(blocks)], axis=1
        )
        for e in range(2)
    ]
    gradients[...] = jnp.concatenate(mine, axis=0).astype(BF16)
    sums = [jnp.zeros((scores.shape[1], LANES), F32) for _ in range(2)]
    at = 0
    for piece in pieces:
        for n in range(piece.shape[0]):
            at += 1
            owner = place[at]
            for b in range(blocks):
                q = piece[n, :, b * LANES : (b + 1) * LANES].astype(F32)
                for e in range(2):
                    sums[e] = sums[e] + q * held[pl.ds(e * rows + owner * blocks + b, 1), :]
    for e in range(2):
        scores[e : e + 1, :] = jnp.sum(sums[e].T, axis=0, keepdims=True)


def finish(place, parts, pieces):
    _, rows, _ = parts.shape
    _, count, width = pieces[0].shape
    return pl.pallas_call(
        finish_kernel,
        out_shape=(shaped((2, width), BF16), shaped((2, count), F32)),
        in_specs=[SMEM, VMEM] + [VMEM] * len(pieces),
        out_specs=(VMEM, VMEM),
        scratch_shapes=[pltpu.VMEM((2 * rows, LANES), F32)],
        compiler_params=pltpu.CompilerParams(vmem_limit_bytes=8 * MIB),
        name="finish",
    )(place, parts, *pieces)


def stops(n_dp, n_tensor):
    chips, side = n_tensor // 2, 4

    def ring(a, n):
        return min(a % n, -a % n)

    shifts = sorted(range(n_dp), key=lambda s: (ring(s // side, side) + ring(s % side, side), s))
    table = np.zeros((n_tensor, n_dp), np.int32)
    for m in range(n_tensor):
        far = sorted(range(n_tensor), key=lambda k: (-ring(k // 2 - m // 2, chips), k))
        for k, shift in zip(far, shifts):
            x, y = (m // side + shift // side) % side, (m % side + shift % side) % side
            table[m, x * side + y] = k
    return table


def local(activations, out_grads, in_factor, out_factor, queries):
    n_dp, n_tensor = lax.axis_size("dp"), lax.axis_size("tensor")
    dp, tensor = lax.axis_index("dp"), lax.axis_index("tensor")
    core = tensor % 2
    chips = n_tensor // 2

    def swapped(x, bits):
        return lax.ppermute(x, "dp", [(i, i ^ bits) for i in range(n_dp)])

    arrays = (activations, out_grads, in_factor, out_factor)
    sent = project((1 - core).reshape(1), *arrays)
    arrived = lax.ppermute(sent, "tensor", [(i, i ^ 1) for i in range(n_tensor)])
    table = stops(n_dp, n_tensor)
    moves = [
        (m * n_tensor + int(table[m, j]), j * n_tensor + m)
        for m in range(n_tensor)
        for j in range(n_dp)
    ]
    turned = lax.ppermute(queries, ("dp", "tensor"), moves)
    kept = project(core.reshape(1), *arrays)
    pair, block = pair_sum(kept, arrived, turned)

    along_z = [[2 * z + c for z in range(chips)] for c in range(2)]
    tokens = pair.shape[0] // chips
    shares = lax.all_to_all(
        pair.reshape(chips, tokens, 2 * RANK), "tensor", 0, 0, axis_index_groups=along_z
    )
    blocks = [block] + [swapped(block, bits) for bits in (1, 2, 3)]
    copies, four = product(shares, n_tensor, blocks)
    everyone = lax.all_to_all(copies, "tensor", 0, 0)
    rest = [swapped(four, 4 * b) for b in range(1, n_dp // 4)]
    order = jnp.asarray(table)[tensor, lax.bitwise_xor(dp, jnp.arange(n_dp))]
    place = jnp.concatenate([tensor.reshape(1), order]).astype(jnp.int32)
    return finish(place, everyone, [four] + rest)


def solution(mesh):
    placed = (
        P("dp", None, "tensor"),
        P("dp", None, "tensor"),
        P(None, "tensor"),
        P(None, "tensor"),
        P("dp", "tensor"),
    )
    return jax.shard_map(
        local,
        mesh=mesh,
        in_specs=placed,
        out_specs=(P("dp", "tensor"), P("dp", "tensor")),
        check_vma=False,
    )
```

time: 167 us -> 55.8 us (0.33); the launches traced: 164 us -> 55.5 us
  blocking collectives: 79.2 us -> 0 us
  waiting for transfers between devices: 57.8 us -> 15.3 us
  starting transfers between devices: 0.04 us -> 28.7 us
  between operations: 14.1 us -> 0.71 us
  Pallas kernels: 0 us -> 10 us
  matrix products: 9.16 us -> 0 us
  local copies, waits for them, and re-layouts: 3.99 us -> 0.67 us
    psum x1 -> x0, blocking collectives: 60.1 us -> none  [local(): summed = lax.psum(paired, 'tensor').astype(jnp.bfloat16)]
    unnamed x2 -> x0, waiting for transfers between devices: 57.8 us -> none
    all_gather x1 -> x0, blocking collectives: 19.1 us -> none  [local(): lax.all_gather(queries, 'dp', axis=0, tiled=True)]
    ppermute x0 -> x8, starting transfers between devices: none -> 15.7 us  [the longest x6 8.79 us: swapped(): return lax.ppermute(x, 'dp', [(i, i ^ bits) for i in range(n_dp)])]
    all_to_all x0 -> x2, starting transfers between devices: none -> 13 us  [the longest x1 8.14 us: local(): lax.all_to_all(pair.reshape(chips, tokens, 2 * RANK), 'tensor', 0, 0, axi...]
    pallas_call x0 -> x5, Pallas kernels: none -> 10 us  [the longest x2 6.73 us: project(): pl.pallas_call(project_kernel, out_shape=pltpu.VMEM((seq, 2 * RANK), F32)...]
    ppermute x0 -> x8, waiting for transfers between devices: none -> 9.24 us  [the longest x6 9.24 us: swapped(): return lax.ppermute(x, 'dp', [(i, i ^ bits) for i in range(n_dp)])]
    dot_general x3 -> x0, matrix products: 8.12 us -> none  [the longest x1 5.4 us: local(): jnp.einsum('esf,rf->esr', activations, in_factor, preferred_element_type=...]
  transfers between devices with their start and end apart: 1 -> 10, of which waited for: 1 -> 6; matrix products, arithmetic and copies ran while one was open for 0% -> 1% of each run, Pallas kernels for 0% -> 6%
where the time goes in v1:
time: 55.8 us; the launch traced here: 55.5 us
  starting transfers between devices  28.7 us (51%)
  waiting for transfers between devices  15.3 us (27%)
  Pallas kernels  10 us (18%)
  between operations  0.71 us (1%)
  local copies, waits for them, and re-layouts  0.67 us (1%)
    ppermute x6, waiting for transfers between devices, swapped(): return lax.ppermute(x, 'dp', [(i, i ^ bits) for i in range(n_dp)])  9.24 us
    ppermute x6, starting transfers between devices, swapped(): return lax.ppermute(x, 'dp', [(i, i ^ bits) for i in range(n_dp)])  8.79 us
    all_to_all x1, starting transfers between devices, local(): lax.all_to_all(pair.reshape(chips, tokens, 2 * RANK), 'tensor', 0, 0, axi...  8.14 us
    pallas_call x2, Pallas kernels, project(): pl.pallas_call(project_kernel, out_shape=pltpu.VMEM((seq, 2 * RANK), F32)...  6.73 us
    all_to_all x1, waiting for transfers between devices, local(): lax.all_to_all(pair.reshape(chips, tokens, 2 * RANK), 'tensor', 0, 0, axi...  6.08 us
    all_to_all x1, starting transfers between devices, local(): everyone = lax.all_to_all(copies, 'tensor', 0, 0)  4.85 us
    ppermute x1, starting transfers between devices, local(): turned = lax.ppermute(queries, ('dp', 'tensor'), moves)  3.63 us
    ppermute x1, starting transfers between devices, local(): lax.ppermute(sent, 'tensor', [(i, i ^ 1) for i in range(n_tensor)])  3.33 us
  transfers between devices with their start and end apart: 10, of which 6 were waited for; matrix products, arithmetic and copies ran while one was open for 1% of the time, Pallas kernels for 6%

profile of v1, /device:TPU:1, one launch (start us, length us, event | category | flops | bytes accessed | tf_op | source)
XLA Modules:
  0.0 55.5 jit_solution(16514045302333584017)
XLA Ops:
  0.6 0.0 copy-start.1
  0.7 3.4 %project.3 = f32[1024,128]{1,0:T(8,128)S(1)} custom-call(s32[1]{0:T(128)} %bitcast.3.which, bf16[2,1024,1792]{2,1,0:T(8,128)(2,1)} %acts.3, bf16[2,1024,512]{2,1,0:T(8,128)(2,1)} %grads.3, bf16[64,1792]{1,0:T(8,128)(2,1)} %inf.3, bf16[64,512]{1,0:T(8,128)(2,1)} %outf.3), custom_call_target="tpu_custom_call" | custom-call | flops 301989888 | bytes 4718592 | tf_op jit(solution)/shard_map/project/pallas_call | solution.py:37
  4.0 0.0 copy-start
  4.1 3.3 %collective-permute-start = (f32[1024,128]{1,0:T(8,128)S(1)}, f32[1024,128]{1,0:T(8,128)S(1)}, u32[]{:S(2)}, u32[]{:S(2)}) collective-permute-start(f32[1024,128]{1,0:T(8,128)S(1)} %project.3), channel_id=1, source_target_pairs={{0,1},{1,0},{2,3},{3,2},{4,5},{5,4},{6,7},{7,6},{8,9},{9,8},{10,11... | collective-permute-start | bytes 1572872 | tf_op jit(solution)/shard_map/ppermute | solution.py:186
  7.4 0.0 copy-done.1
  7.4 3.6 %collective-permute-start.1 = (bf16[64,256]{1,0:T(8,128)(2,1)S(1)}, bf16[64,256]{1,0:T(8,128)(2,1)S(1)}, u32[]{:S(2)}, u32[]{:S(2)}) collective-permute-start(bf16[64,256]{1,0:T(8,128)(2,1)S(1)} %copy-done.1), channel_id=1, source_target_pairs={{8,0},{9,16},{11,32},{6,48},{7,64},{4,80},{3,96},{5,112},{12,128},... | collective-permute-start | bytes 98312 | tf_op jit(solution)/shard_map/ppermute | solution.py:193
  11.0 3.4 %project.2.kept = f32[1024,128]{1,0:T(8,128)S(1)} custom-call(s32[1]{0:T(128)} %bitcast.2.which, bf16[2,1024,1792]{2,1,0:T(8,128)(2,1)} %acts.3, bf16[2,1024,512]{2,1,0:T(8,128)(2,1)} %grads.3, bf16[64,1792]{1,0:T(8,128)(2,1)} %inf.3, bf16[64,512]{1,0:T(8,128)(2,1)} %outf.3), custom_call_target="tpu_custom_call" | custom-call | flops 301989888 | bytes 4718592 | tf_op jit(solution)/shard_map/project/pallas_call | solution.py:37
  14.4 0.0 collective-permute-done.1.block
  14.4 0.0 collective-permute-done.arrived
  14.4 0.8 %pair_sum.1 = (bf16[1024,128]{1,0:T(8,128)(2,1)}, bf16[64,256]{1,0:T(8,128)(2,1)S(1)}) custom-call(f32[1024,128]{1,0:T(8,128)S(1)} %project.2.kept, f32[1024,128]{1,0:T(8,128)S(1)} %collective-permute-done.arrived, bf16[64,256]{1,0:T(8,128)(2,1)S(1)} %collective-permute-done.1.block), custom_call_target="tpu_custom_call" | custom-call | tf_op jit(solution)/shard_map/pair_sum/pallas_call | solution.py:67
  15.1 8.1 %all-to-all-start = ((bf16[8,128,128]{2,1,0:T(8,128)(2,1)}), bf16[8,128,128]{2,1,0:T(8,128)(2,1)S(1)}, u32[]{:S(2)}, u32[]{:S(2)}) async-start(bf16[8,128,128]{2,1,0:T(8,128)(2,1)} %bitcast.4), calls=%async_computation | async-start | bytes 524288 | tf_op jit(solution)/shard_map/all_to_all | solution.py:199
  23.3 0.0 collective-permute-start.2
  23.3 2.1 %collective-permute-start.3 = (bf16[64,256]{1,0:T(8,128)(2,1)S(1)}, bf16[64,256]{1,0:T(8,128)(2,1)S(1)}, u32[]{:S(2)}, u32[]{:S(2)}) collective-permute-start(bf16[64,256]{1,0:T(8,128)(2,1)S(1)} %get-tuple-element.7.refs_0_), channel_id=1, source_target_pairs={{0,32},{16,48},{32,0},{48,16},{64,96},{80,112},{96,64},{112,80},{1... | collective-permute-start | bytes 98312 | tf_op jit(solution)/shard_map/ppermute | solution.py:182
  25.4 1.8 %collective-permute-start.4 = (bf16[64,256]{1,0:T(8,128)(2,1)S(1)}, bf16[64,256]{1,0:T(8,128)(2,1)S(1)}, u32[]{:S(2)}, u32[]{:S(2)}) collective-permute-start(bf16[64,256]{1,0:T(8,128)(2,1)S(1)} %get-tuple-element.7.refs_0_), channel_id=1, source_target_pairs={{0,48},{16,32},{32,16},{48,0},{64,112},{80,96},{96,80},{112,64},{1... | collective-permute-start | bytes 98312 | tf_op jit(solution)/shard_map/ppermute | solution.py:182
  27.1 0.0 collective-permute-done.2.refs_1_
  27.2 0.5 collective-permute-done.3.refs_2_
  27.7 2.0 %collective-permute-done.4.refs_3_ = bf16[64,256]{1,0:T(8,128)(2,1)S(1)} collective-permute-done((bf16[64,256]{1,0:T(8,128)(2,1)S(1)}, bf16[64,256]{1,0:T(8,128)(2,1)S(1)}, u32[]{:S(2)}, u32[]{:S(2)}) %collective-permute-start.4) | collective-permute-done | bytes 32800 | tf_op jit(solution)/shard_map/ppermute | solution.py:182
  29.6 6.1 %all-to-all-done.parts = bf16[8,128,128]{2,1,0:T(8,128)(2,1)S(1)} async-done(((bf16[8,128,128]{2,1,0:T(8,128)(2,1)}), bf16[8,128,128]{2,1,0:T(8,128)(2,1)S(1)}, u32[]{:S(2)}, u32[]{:S(2)}) %all-to-all-start) | async-done | bytes 262176 | tf_op jit(solution)/shard_map/all_to_all | solution.py:199
  35.7 1.1 %product.1 = (f32[16,32,128]{2,1,0:T(8,128)}, bf16[4,64,256]{2,1,0:T(8,128)(2,1)S(1)}) custom-call(bf16[8,128,128]{2,1,0:T(8,128)(2,1)S(1)} %all-to-all-done.parts, bf16[64,256]{1,0:T(8,128)(2,1)S(1)} %get-tuple-element.7.refs_0_, bf16[64,256]{1,0:T(8,128)(2,1)S(1)} %collective-permute-done.2.refs_1_, bf16[64,256]{1,0:T(8,128)(2,1)S(1)} %collective-permute-done.3.refs_2_, ...), custom_call_target="tpu_custom_call" | custom-call | tf_op jit(solution)/shard_map/product/pallas_call | solution.py:99
  36.8 4.9 %all-to-all-start.1 = ((f32[16,32,128]{2,1,0:T(8,128)}), f32[16,32,128]{2,1,0:T(8,128)S(1)}, u32[]{:S(2)}, u32[]{:S(2)}) async-start(f32[16,32,128]{2,1,0:T(8,128)} %get-tuple-element.8), calls=%async_computation.1 | async-start | bytes 524288 | tf_op jit(solution)/shard_map/all_to_all | solution.py:204
  41.7 2.4 %collective-permute-start.5 = (bf16[4,64,256]{2,1,0:T(8,128)(2,1)S(1)}, bf16[4,64,256]{2,1,0:T(8,128)(2,1)S(1)}, u32[]{:S(2)}, u32[]{:S(2)}) collective-permute-start(bf16[4,64,256]{2,1,0:T(8,128)(2,1)S(1)} %get-tuple-element.9.refs_0_), channel_id=1, source_target_pairs={{0,64},{16,80},{32,96},{48,112},{64,0},{80,16},{96,32},{112,48},{1... | collective-permute-start | bytes 393224 | tf_op jit(solution)/shard_map/ppermute | solution.py:182
  44.1 1.2 %collective-permute-start.6 = (bf16[4,64,256]{2,1,0:T(8,128)(2,1)S(1)}, bf16[4,64,256]{2,1,0:T(8,128)(2,1)S(1)}, u32[]{:S(2)}, u32[]{:S(2)}) collective-permute-start(bf16[4,64,256]{2,1,0:T(8,128)(2,1)S(1)} %get-tuple-element.9.refs_0_), channel_id=1, source_target_pairs={{0,128},{16,144},{32,160},{48,176},{64,192},{80,208},{96,224},{112... | collective-permute-start | bytes 393224 | tf_op jit(solution)/shard_map/ppermute | solution.py:182
  45.3 1.3 %collective-permute-start.7 = (bf16[4,64,256]{2,1,0:T(8,128)(2,1)S(1)}, bf16[4,64,256]{2,1,0:T(8,128)(2,1)S(1)}, u32[]{:S(2)}, u32[]{:S(2)}) collective-permute-start(bf16[4,64,256]{2,1,0:T(8,128)(2,1)S(1)} %get-tuple-element.9.refs_0_), channel_id=1, source_target_pairs={{0,192},{16,208},{32,224},{48,240},{64,128},{80,144},{96,160},{112... | collective-permute-start | bytes 393224 | tf_op jit(solution)/shard_map/ppermute | solution.py:182
  46.6 0.0 copy-done
  46.6 0.7 %gather_fusion = s32[16]{0:T(128)S(1)} fusion(s32[16,16]{1,0:T(8,128)S(1)} %copy-done, s32[16]{0:T(128)S(1)} %fusion.3), kind=kCustom, calls=%fused_computation | custom fusion | bytes 256 | tf_op jit(solution)/shard_map/gather | solution.py:206
  47.3 0.1 pad_add_fusion.place
  47.3 0.5 collective-permute-done.5.refs_1_
  47.9 3.7 %collective-permute-done.6.refs_2_ = bf16[4,64,256]{2,1,0:T(8,128)(2,1)S(1)} collective-permute-done((bf16[4,64,256]{2,1,0:T(8,128)(2,1)S(1)}, bf16[4,64,256]{2,1,0:T(8,128)(2,1)S(1)}, u32[]{:S(2)}, u32[]{:S(2)}) %collective-permute-start.6) | collective-permute-done | bytes 131104 | tf_op jit(solution)/shard_map/ppermute | solution.py:182
  51.6 2.5 %collective-permute-done.7.refs_3_ = bf16[4,64,256]{2,1,0:T(8,128)(2,1)S(1)} collective-permute-done((bf16[4,64,256]{2,1,0:T(8,128)(2,1)S(1)}, bf16[4,64,256]{2,1,0:T(8,128)(2,1)S(1)}, u32[]{:S(2)}, u32[]{:S(2)}) %collective-permute-start.7) | collective-permute-done | bytes 131104 | tf_op jit(solution)/shard_map/ppermute | solution.py:182
  54.1 0.0 all-to-all-done.1.parts
  54.1 1.4 %finish.1 = (bf16[2,256]{1,0:T(2,128)(2,1)}, f32[2,64]{1,0:T(2,128)}) custom-call(s32[17]{0:T(128)S(1)} %pad_add_fusion.place, f32[16,32,128]{2,1,0:T(8,128)S(1)} %all-to-all-done.1.parts, bf16[4,64,256]{2,1,0:T(8,128)(2,1)S(1)} %get-tuple-element.9.refs_0_, bf16[4,64,256]{2,1,0:T(8,128)(2,1)S(1)} %collective-permute-done.5.refs_1_, ...), custom_call_target="tpu_custom_call" | custom-call | tf_op jit(solution)/shard_map/finish/pallas_call | solution.py:148
  (1 shorter events, 0.0 us)
Async XLA Ops:
  0.6 6.8 %copy-start.1 = (bf16[64,256]{1,0:T(8,128)(2,1)S(1)}, bf16[64,256]{1,0:T(8,128)(2,1)}, u32[]{:S(2)}) copy-start(bf16[64,256]{1,0:T(8,128)(2,1)} %param.10) | copy-start | bytes 98308
  4.0 42.6 %copy-start = (s32[16,16]{1,0:T(8,128)S(1)}, s32[16,16]{1,0:T(8,128)}, u32[]{:S(2)}) copy-start(s32[16,16]{1,0:T(8,128)} %constant.28.clone) | copy-start | bytes 3076
  4.1 10.3 %collective-permute-start = (f32[1024,128]{1,0:T(8,128)S(1)}, f32[1024,128]{1,0:T(8,128)S(1)}, u32[]{:S(2)}, u32[]{:S(2)}) collective-permute-start(f32[1024,128]{1,0:T(8,128)S(1)} %project.3), channel_id=1, source_target_pairs={{0,1},{1,0},{2,3},{3,2},{4,5},{5,4},{6,7},{7,6},{8,9},{9,8},{10,11... | collective-permute-start | bytes 1572872 | tf_op jit(solution)/shard_map/ppermute | solution.py:186
  7.4 7.0 %collective-permute-start.1 = (bf16[64,256]{1,0:T(8,128)(2,1)S(1)}, bf16[64,256]{1,0:T(8,128)(2,1)S(1)}, u32[]{:S(2)}, u32[]{:S(2)}) collective-permute-start(bf16[64,256]{1,0:T(8,128)(2,1)S(1)} %copy-done.1), channel_id=1, source_target_pairs={{8,0},{9,16},{11,32},{6,48},{7,64},{4,80},{3,96},{5,112},{12,128},... | collective-permute-start | bytes 98312 | tf_op jit(solution)/shard_map/ppermute | solution.py:193
  15.1 20.6 %all-to-all-start = ((bf16[8,128,128]{2,1,0:T(8,128)(2,1)}), bf16[8,128,128]{2,1,0:T(8,128)(2,1)S(1)}, u32[]{:S(2)}, u32[]{:S(2)}) async-start(bf16[8,128,128]{2,1,0:T(8,128)(2,1)} %bitcast.4), calls=%async_computation | async-start | bytes 524288 | tf_op jit(solution)/shard_map/all_to_all | solution.py:199
  23.3 3.9 %collective-permute-start.2 = (bf16[64,256]{1,0:T(8,128)(2,1)S(1)}, bf16[64,256]{1,0:T(8,128)(2,1)S(1)}, u32[]{:S(2)}, u32[]{:S(2)}) collective-permute-start(bf16[64,256]{1,0:T(8,128)(2,1)S(1)} %get-tuple-element.7.refs_0_), channel_id=1, source_target_pairs={{0,16},{16,0},{32,48},{48,32},{64,80},{80,64},{96,112},{112,96},{1... | collective-permute-start | bytes 98312 | tf_op jit(solution)/shard_map/ppermute | solution.py:182
  23.3 4.4 %collective-permute-start.3 = (bf16[64,256]{1,0:T(8,128)(2,1)S(1)}, bf16[64,256]{1,0:T(8,128)(2,1)S(1)}, u32[]{:S(2)}, u32[]{:S(2)}) collective-permute-start(bf16[64,256]{1,0:T(8,128)(2,1)S(1)} %get-tuple-element.7.refs_0_), channel_id=1, source_target_pairs={{0,32},{16,48},{32,0},{48,16},{64,96},{80,112},{96,64},{112,80},{1... | collective-permute-start | bytes 98312 | tf_op jit(solution)/shard_map/ppermute | solution.py:182
  25.4 4.3 %collective-permute-start.4 = (bf16[64,256]{1,0:T(8,128)(2,1)S(1)}, bf16[64,256]{1,0:T(8,128)(2,1)S(1)}, u32[]{:S(2)}, u32[]{:S(2)}) collective-permute-start(bf16[64,256]{1,0:T(8,128)(2,1)S(1)} %get-tuple-element.7.refs_0_), channel_id=1, source_target_pairs={{0,48},{16,32},{32,16},{48,0},{64,112},{80,96},{96,80},{112,64},{1... | collective-permute-start | bytes 98312 | tf_op jit(solution)/shard_map/ppermute | solution.py:182
  36.8 17.3 %all-to-all-start.1 = ((f32[16,32,128]{2,1,0:T(8,128)}), f32[16,32,128]{2,1,0:T(8,128)S(1)}, u32[]{:S(2)}, u32[]{:S(2)}) async-start(f32[16,32,128]{2,1,0:T(8,128)} %get-tuple-element.8), calls=%async_computation.1 | async-start | bytes 524288 | tf_op jit(solution)/shard_map/all_to_all | solution.py:204
  41.7 6.2 %collective-permute-start.5 = (bf16[4,64,256]{2,1,0:T(8,128)(2,1)S(1)}, bf16[4,64,256]{2,1,0:T(8,128)(2,1)S(1)}, u32[]{:S(2)}, u32[]{:S(2)}) collective-permute-start(bf16[4,64,256]{2,1,0:T(8,128)(2,1)S(1)} %get-tuple-element.9.refs_0_), channel_id=1, source_target_pairs={{0,64},{16,80},{32,96},{48,112},{64,0},{80,16},{96,32},{112,48},{1... | collective-permute-start | bytes 393224 | tf_op jit(solution)/shard_map/ppermute | solution.py:182
  44.1 7.5 %collective-permute-start.6 = (bf16[4,64,256]{2,1,0:T(8,128)(2,1)S(1)}, bf16[4,64,256]{2,1,0:T(8,128)(2,1)S(1)}, u32[]{:S(2)}, u32[]{:S(2)}) collective-permute-start(bf16[4,64,256]{2,1,0:T(8,128)(2,1)S(1)} %get-tuple-element.9.refs_0_), channel_id=1, source_target_pairs={{0,128},{16,144},{32,160},{48,176},{64,192},{80,208},{96,224},{112... | collective-permute-start | bytes 393224 | tf_op jit(solution)/shard_map/ppermute | solution.py:182
  45.3 8.8 %collective-permute-start.7 = (bf16[4,64,256]{2,1,0:T(8,128)(2,1)S(1)}, bf16[4,64,256]{2,1,0:T(8,128)(2,1)S(1)}, u32[]{:S(2)}, u32[]{:S(2)}) collective-permute-start(bf16[4,64,256]{2,1,0:T(8,128)(2,1)S(1)} %get-tuple-element.9.refs_0_), channel_id=1, source_target_pairs={{0,192},{16,208},{32,224},{48,240},{64,128},{80,144},{96,160},{112... | collective-permute-start | bytes 393224 | tf_op jit(solution)/shard_map/ppermute | solution.py:182

commit v2 on v1

v2 whole, which is shorter than its diff:
```python
import jax
import jax.numpy as jnp
from jax import lax
from jax.experimental import pallas as pl
from jax.experimental.pallas import tpu as pltpu
from jax.sharding import PartitionSpec as P

RANK = 64
LANES = 128
F32 = jnp.float32
BF16 = jnp.bfloat16
MIB = 1024 * 1024
FORWARD = 20000000000
HOLD = 1000000000
SENT = jnp.bfloat16
NT = (((1,), (1,)), ((), ()))
TN = (((0,), (0,)), ((), ()))
SMEM = pl.BlockSpec(memory_space=pltpu.SMEM)
VMEM = pl.BlockSpec(memory_space=pltpu.VMEM)
ANY = pl.BlockSpec(memory_space=pl.ANY)


def shaped(shape, dtype):
    return jax.ShapeDtypeStruct(shape, dtype)


def project_kernel(which, acts, grads, inf, outf, block, out, same):
    del which
    same[...] = block[...]
    left = lax.dot_general(acts[0], inf[...], NT, preferred_element_type=F32)
    right = lax.dot_general(grads[0], outf[...], NT, preferred_element_type=F32)
    out[...] = jnp.concatenate([left, right], axis=1)


def project(which, acts, grads, inf, outf, block):
    _, seq, ff = acts.shape
    d = grads.shape[2]
    rows = seq // 2
    held = [
        pltpu.with_memory_space_constraint(x, pltpu.HBM) for x in (acts, grads, inf, outf, block)
    ]
    return pl.pallas_call(
        project_kernel,
        out_shape=(
            pltpu.VMEM((seq, 2 * RANK), F32),
            pltpu.VMEM(block.shape, block.dtype),
        ),
        grid_spec=pltpu.PrefetchScalarGridSpec(
            num_scalar_prefetch=1,
            grid=(seq // rows,),
            in_specs=[
                pl.BlockSpec((1, rows, ff), lambda i, w: (w[0], i, 0)),
                pl.BlockSpec((1, rows, d), lambda i, w: (w[0], i, 0)),
                pl.BlockSpec((RANK, ff), lambda i, w: (0, 0)),
                pl.BlockSpec((RANK, d), lambda i, w: (0, 0)),
                pl.BlockSpec(block.shape, lambda i, w: (0, 0)),
            ],
            out_specs=(
                pl.BlockSpec((rows, 2 * RANK), lambda i, w: (i, 0)),
                pl.BlockSpec(block.shape, lambda i, w: (0, 0)),
            ),
        ),
        compiler_params=pltpu.CompilerParams(vmem_limit_bytes=24 * MIB),
        cost_estimate=pl.CostEstimate(
            flops=20 * seq * (ff + d) * RANK,
            bytes_accessed=2 * seq * (ff + d),
            transcendentals=0,
        ),
        name="project",
    )(which, *held)


def whole_kernel(which, acts, grads, inf, outf, out):
    left = lax.dot_general(acts[which[0]], inf[...], NT, preferred_element_type=F32)
    right = lax.dot_general(grads[which[0]], outf[...], NT, preferred_element_type=F32)
    out[...] = jnp.concatenate([left, right], axis=1)


def project_whole(which, acts, grads, inf, outf):
    _, seq, ff = acts.shape
    d = grads.shape[2]
    held = [pltpu.with_memory_space_constraint(x, pltpu.VMEM) for x in (acts, grads, inf, outf)]
    return pl.pallas_call(
        whole_kernel,
        out_shape=pltpu.VMEM((seq, 2 * RANK), F32),
        in_specs=[SMEM, VMEM, VMEM, VMEM, VMEM],
        out_specs=VMEM,
        compiler_params=pltpu.CompilerParams(vmem_limit_bytes=24 * MIB),
        cost_estimate=pl.CostEstimate(
            flops=1 * 2 * seq * (ff + d) * RANK,
            bytes_accessed=2 * seq * (ff + d),
            transcendentals=0,
        ),
        name="project_whole",
    )(which, *held)


def pair_kernel(kept, arrived, out):
    out[...] = (kept[...] + arrived[...]).astype(BF16)


def pair_sum(kept, arrived):
    return pl.pallas_call(
        pair_kernel,
        out_shape=shaped(kept.shape, BF16),
        in_specs=[VMEM] * 2,
        out_specs=VMEM,
        compiler_params=pltpu.CompilerParams(vmem_limit_bytes=8 * MIB),
        name="pair_sum",
    )(kept, arrived)


def forward_kernel(block, after, out):
    del after
    out[...] = block[...]


def forward(block, after):
    return pl.pallas_call(
        forward_kernel,
        out_shape=shaped(block.shape, block.dtype),
        in_specs=[VMEM, ANY],
        out_specs=VMEM,
        compiler_params=pltpu.CompilerParams(vmem_limit_bytes=8 * MIB),
        cost_estimate=pl.CostEstimate(flops=FORWARD, bytes_accessed=0, transcendentals=0),
        name="forward",
    )(block, after)


def join_kernel(*refs):
    out = refs[-1]
    for n, block in enumerate(refs[:-1]):
        out[n] = block[...]


def join(blocks):
    return pl.pallas_call(
        join_kernel,
        out_shape=shaped((len(blocks),) + blocks[0].shape, BF16),
        in_specs=[VMEM] * len(blocks),
        out_specs=VMEM,
        compiler_params=pltpu.CompilerParams(vmem_limit_bytes=8 * MIB),
        name="join",
    )(*blocks)


def hold_kernel(place, after, out):
    del after
    for n in range(place.shape[0]):
        out[n] = place[n]


def hold(place, after):
    return pl.pallas_call(
        hold_kernel,
        out_shape=shaped(place.shape, place.dtype),
        in_specs=[SMEM, ANY],
        out_specs=SMEM,
        cost_estimate=pl.CostEstimate(flops=HOLD, bytes_accessed=0, transcendentals=0),
        compiler_params=pltpu.CompilerParams(vmem_limit_bytes=8 * MIB),
        name="hold",
    )(place, after)


def product_kernel(parts, queries, out, same, square):
    total = jnp.sum(parts[...].astype(F32), axis=0)
    square[...] = lax.dot_general(
        total[:, :RANK],
        total[:, RANK:],
        TN,
        precision=lax.Precision.HIGHEST,
        preferred_element_type=F32,
    )
    half = RANK // 2
    rows = jnp.concatenate(
        [square[pl.ds(0, half, stride=2), :], square[pl.ds(1, half, stride=2), :]], axis=1
    ).astype(out.dtype)
    for copy in range(out.shape[0]):
        out[copy] = rows
    same[...] = queries[...]


def product(parts, copies, queries):
    return pl.pallas_call(
        product_kernel,
        out_shape=(
            shaped((copies, RANK * RANK // LANES, LANES), SENT),
            shaped(queries.shape, queries.dtype),
        ),
        in_specs=[VMEM, VMEM],
        out_specs=(VMEM, VMEM),
        scratch_shapes=[pltpu.VMEM((RANK, RANK), F32)],
        compiler_params=pltpu.CompilerParams(vmem_limit_bytes=8 * MIB),
        name="product",
    )(parts, queries)


def finish_kernel(place, parts, *refs):
    pieces = refs[:-3]
    gradients, scores, held = refs[-3:]
    dp, tensor = place[0], place[1]
    near = near_stops(parts.shape[0])
    halves = [sum(r << (4 * n) for n, r in enumerate(near[at : at + 8])) for at in (0, 8)]
    halves = [jnp.int32(h - (1 << 32) if h >> 31 else h) for h in halves]

    def lookup(shift):
        half = jnp.where(shift < 8, halves[0], halves[1])
        return lax.shift_right_logical(half, 4 * (shift & 7)) & 15

    devices, rows, _ = parts.shape
    for example in range(2):
        total = parts[example].astype(F32)
        for z in range(1, devices // 2):
            total = total + parts[2 * z + example].astype(F32)
        held[example * rows : (example + 1) * rows] = total.astype(BF16).astype(F32)
    blocks = rows // devices
    mine = [
        jnp.concatenate(
            [held[pl.ds(e * rows + tensor * blocks + b, 1), :] for b in range(blocks)], axis=1
        )
        for e in range(2)
    ]
    gradients[...] = jnp.concatenate(mine, axis=0).astype(BF16)
    sums = [jnp.zeros((scores.shape[1], LANES), F32) for _ in range(2)]
    at = 0
    for piece in pieces:
        for n in range(piece.shape[0]):
            owner = source(tensor, lax.bitwise_xor(dp, jnp.int32(at)), lookup)
            at += 1
            for b in range(blocks):
                q = piece[n, :, b * LANES : (b + 1) * LANES].astype(F32)
                for e in range(2):
                    sums[e] = sums[e] + q * held[pl.ds(e * rows + owner * blocks + b, 1), :]
    for e in range(2):
        scores[e : e + 1, :] = jnp.sum(sums[e].T, axis=0, keepdims=True)


def finish(place, parts, pieces):
    _, rows, _ = parts.shape
    _, count, width = pieces[0].shape
    return pl.pallas_call(
        finish_kernel,
        out_shape=(shaped((2, width), BF16), shaped((2, count), F32)),
        in_specs=[SMEM, VMEM] + [VMEM] * len(pieces),
        out_specs=(VMEM, VMEM),
        scratch_shapes=[pltpu.VMEM((2 * rows, LANES), F32)],
        compiler_params=pltpu.CompilerParams(vmem_limit_bytes=8 * MIB),
        name="finish",
    )(place, parts, *pieces)


def ring(a, n):
    return min(a % n, -a % n)


def near_stops(n_tensor):
    shifts = sorted(range(16), key=lambda s: (ring(s // 4, 4) + ring(s % 4, 4), s))
    far = sorted(range(n_tensor), key=lambda r: (-ring(r // 2, n_tensor // 2), r))
    return [r for _, r in sorted(zip(shifts, far))]


def source(m, j, lookup):
    shift = (((j >> 2) - (m >> 2)) & 3) * 4 + ((j - m) & 3)
    r = lookup(shift)
    return (((m >> 1) + (r >> 1)) & 7) * 2 + (r & 1)


def local(activations, out_grads, in_factor, out_factor, queries):
    n_dp, n_tensor = lax.axis_size("dp"), lax.axis_size("tensor")
    dp, tensor = lax.axis_index("dp"), lax.axis_index("tensor")
    core = tensor % 2
    chips = n_tensor // 2

    def swapped(x, bits):
        return lax.ppermute(x, "dp", [(i, i ^ bits) for i in range(n_dp)])

    arrays = (activations, out_grads, in_factor, out_factor)
    sent, block = project((1 - core).reshape(1), *arrays, queries)
    arrived = lax.ppermute(sent, "tensor", [(i, i ^ 1) for i in range(n_tensor)])
    near = near_stops(n_tensor)
    moves = [
        (m * n_tensor + source(m, j, near.__getitem__), j * n_tensor + m)
        for m in range(n_tensor)
        for j in range(n_dp)
    ]
    turned = lax.ppermute(block, ("dp", "tensor"), moves)
    kept = project_whole(core.reshape(1), *arrays)
    pair = pair_sum(kept, arrived)
    block = forward(turned, pair)

    along_z = [[2 * z + c for z in range(chips)] for c in range(2)]
    tokens = pair.shape[0] // chips
    shares = lax.all_to_all(
        pair.reshape(chips, tokens, 2 * RANK), "tensor", 0, 0, axis_index_groups=along_z
    )
    four = join([block] + [swapped(block, bits) for bits in (1, 2, 3)])
    two = swapped(four, 8)
    copies, same = product(shares, n_tensor, four)
    everyone = lax.all_to_all(copies, "tensor", 0, 0)
    one, three = swapped(same, 4), swapped(same, 12)
    place = hold(jnp.stack([dp, tensor]).astype(jnp.int32), two)
    return finish(place, everyone, [same, one, two, three])


def solution(mesh):
    placed = (
        P("dp", None, "tensor"),
        P("dp", None, "tensor"),
        P(None, "tensor"),
        P(None, "tensor"),
        P("dp", "tensor"),
    )
    return jax.shard_map(
        local,
        mesh=mesh,
        in_specs=placed,
        out_specs=(P("dp", "tensor"), P("dp", "tensor")),
        check_vma=False,
    )
```

time: 55.8 us -> 48.1 us (0.86)
  waiting for transfers between devices: 15.3 us -> 11.3 us
  starting transfers between devices: 28.7 us -> 26.2 us
  local copies, waits for them, and re-layouts: 0.67 us -> 0.02 us
    all_to_all x1, starting transfers between devices: 8.14 us -> 3.77 us  [local(): lax.all_to_all(pair.reshape(chips, tokens, 2 * RANK), 'tensor', 0, 0, axi...]
    all_to_all x1, waiting for transfers between devices: 6.08 us -> 2.03 us  [local(): lax.all_to_all(pair.reshape(chips, tokens, 2 * RANK), 'tensor', 0, 0, axi...]
    all_to_all x1, starting transfers between devices: 4.85 us -> 7.57 us  [local(): everyone = lax.all_to_all(copies, 'tensor', 0, 0)]
    gather x1 -> x0, local copies, waits for them, and re-layouts: 0.66 us -> none  [local(): order = jnp.asarray(table)[tensor, lax.bitwise_xor(dp, jnp.arange(n_dp))]]
    ppermute x6, starting transfers between devices: 8.79 us -> 8.17 us  [swapped(): return lax.ppermute(x, 'dp', [(i, i ^ bits) for i in range(n_dp)])]
    pallas_call x3 -> x6, Pallas kernels: 7.48 us -> 7.13 us  [the longest x1 3.81 us: project(): pl.pallas_call(project_kernel, out_shape=(pltpu.VMEM((seq, 2 * RANK), F32...]
  transfers between devices with their start and end apart: 10 -> 10, of which waited for: 6 -> 5; matrix products, arithmetic and copies ran while one was open for 1% -> 0% of each run, Pallas kernels for 6% -> 7%
where the time goes in v2:
time: 48.1 us; the launch traced here: 47.9 us
  starting transfers between devices  26.2 us (54%)
  waiting for transfers between devices  11.3 us (23%)
  Pallas kernels  9.58 us (20%)
  between operations  0.73 us (2%)
    ppermute x6, waiting for transfers between devices, swapped(): return lax.ppermute(x, 'dp', [(i, i ^ bits) for i in range(n_dp)])  9.22 us
    ppermute x6, starting transfers between devices, swapped(): return lax.ppermute(x, 'dp', [(i, i ^ bits) for i in range(n_dp)])  8.17 us
    all_to_all x1, starting transfers between devices, local(): everyone = lax.all_to_all(copies, 'tensor', 0, 0)  7.57 us
    pallas_call x1, Pallas kernels, project(): pl.pallas_call(project_kernel, out_shape=(pltpu.VMEM((seq, 2 * RANK), F32...  3.81 us
    all_to_all x1, starting transfers between devices, local(): lax.all_to_all(pair.reshape(chips, tokens, 2 * RANK), 'tensor', 0, 0, axi...  3.77 us
    ppermute x1, starting transfers between devices, local(): turned = lax.ppermute(block, ('dp', 'tensor'), moves)  3.61 us
    ppermute x1, starting transfers between devices, local(): lax.ppermute(sent, 'tensor', [(i, i ^ 1) for i in range(n_tensor)])  3.08 us
    all_to_all x1, waiting for transfers between devices, local(): lax.all_to_all(pair.reshape(chips, tokens, 2 * RANK), 'tensor', 0, 0, axi...  2.03 us
  transfers between devices with their start and end apart: 10, of which 5 were waited for; matrix products, arithmetic and copies ran while one was open for 0% of the time, Pallas kernels for 7%

profile of v2, /device:TPU:1, one launch (start us, length us, event | category | flops | bytes accessed | tf_op | source)
XLA Modules:
  0.0 47.9 jit_solution(2195975011337234637)
XLA Ops:
  0.6 0.0 copy-start.1
  0.6 0.0 copy-start.2
  0.7 0.0 copy-start.3
  0.7 0.0 copy-start
  0.7 3.8 %project.1 = (f32[1024,128]{1,0:T(8,128)S(1)}, bf16[64,256]{1,0:T(8,128)(2,1)S(1)}) custom-call(s32[1]{0:T(128)} %bitcast.2.which, bf16[2,1024,1792]{2,1,0:T(8,128)(2,1)} %acts.3, bf16[2,1024,512]{2,1,0:T(8,128)(2,1)} %grads.3, bf16[64,1792]{1,0:T(8,128)(2,1)} %inf.3, bf16[64,512]{1,0:T(8,128)(2,1)} %outf.3, bf16[64,256]{1,0:T(8,128)(2,1)} %block.1), custom_call_target="tpu_custom_call" | custom-call | flops 3019898880 | bytes 4718592 | tf_op jit(solution)/shard_map/project/pallas_call | solution.py:42
  4.5 3.1 %collective-permute-start.1 = (f32[1024,128]{1,0:T(8,128)S(1)}, f32[1024,128]{1,0:T(8,128)S(1)}, u32[]{:S(2)}, u32[]{:S(2)}) collective-permute-start(f32[1024,128]{1,0:T(8,128)S(1)} %get-tuple-element.7), channel_id=1, source_target_pairs={{0,1},{1,0},{2,3},{3,2},{4,5},{5,4},{6,7},{7,6},{8,9},{9,8},{10,11... | collective-permute-start | bytes 1572872 | tf_op jit(solution)/shard_map/ppermute | solution.py:279
  7.6 3.6 %collective-permute-start = (bf16[64,256]{1,0:T(8,128)(2,1)S(1)}, bf16[64,256]{1,0:T(8,128)(2,1)S(1)}, u32[]{:S(2)}, u32[]{:S(2)}) collective-permute-start(bf16[64,256]{1,0:T(8,128)(2,1)S(1)} %get-tuple-element.6), channel_id=1, source_target_pairs={{8,0},{9,16},{11,32},{6,48},{7,64},{4,80},{3,96},{5,112},{12,128},... | collective-permute-start | bytes 98312 | tf_op jit(solution)/shard_map/ppermute | solution.py:286
  11.2 0.0 copy-done.1
  11.2 0.0 copy-done.2
  11.2 0.0 copy-done.3
  11.2 0.0 copy-done
  11.2 1.4 %project_whole.1.kept = f32[1024,128]{1,0:T(8,128)S(1)} custom-call(s32[1]{0:T(128)} %bitcast.3.which, bf16[2,1024,1792]{2,1,0:T(8,128)(2,1)S(1)} %copy-done, bf16[2,1024,512]{2,1,0:T(8,128)(2,1)S(1)} %copy-done.1, bf16[64,1792]{1,0:T(8,128)(2,1)S(1)} %copy-done.2, bf16[64,512]{1,0:T(8,128)(2,1)S(1)} %copy-done.3), custom_call_target="tpu_custom_call" | custom-call | flops 301989888 | bytes 4718592 | tf_op jit(solution)/shard_map/project_whole/pallas_call | solution.py:83
  12.6 0.0 collective-permute-done.1.arrived
  12.7 0.7 %pair_sum.1.after = bf16[1024,128]{1,0:T(8,128)(2,1)} custom-call(f32[1024,128]{1,0:T(8,128)S(1)} %project_whole.1.kept, f32[1024,128]{1,0:T(8,128)S(1)} %collective-permute-done.1.arrived), custom_call_target="tpu_custom_call" | custom-call | tf_op jit(solution)/shard_map/pair_sum/pallas_call | solution.py:103
  13.4 3.8 %all-to-all-start = ((bf16[8,128,128]{2,1,0:T(8,128)(2,1)}), bf16[8,128,128]{2,1,0:T(8,128)(2,1)S(1)}, u32[]{:S(2)}, u32[]{:S(2)}) async-start(bf16[8,128,128]{2,1,0:T(8,128)(2,1)} %bitcast.4), calls=%async_computation | async-start | bytes 524288 | tf_op jit(solution)/shard_map/all_to_all | solution.py:293
  17.2 0.0 collective-permute-done.block
  17.2 1.4 %collective-permute-start.2 = (bf16[64,256]{1,0:T(8,128)(2,1)S(1)}, bf16[64,256]{1,0:T(8,128)(2,1)S(1)}, u32[]{:S(2)}, u32[]{:S(2)}) collective-permute-start(bf16[64,256]{1,0:T(8,128)(2,1)S(1)} %forward.1.refs_0_), channel_id=1, source_target_pairs={{0,16},{16,0},{32,48},{48,32},{64,80},{80,64},{96,112},{112,96},{1... | collective-permute-start | bytes 98312 | tf_op jit(solution)/shard_map/ppermute | solution.py:275
  18.6 2.6 %collective-permute-start.3 = (bf16[64,256]{1,0:T(8,128)(2,1)S(1)}, bf16[64,256]{1,0:T(8,128)(2,1)S(1)}, u32[]{:S(2)}, u32[]{:S(2)}) collective-permute-start(bf16[64,256]{1,0:T(8,128)(2,1)S(1)} %forward.1.refs_0_), channel_id=1, source_target_pairs={{0,32},{16,48},{32,0},{48,16},{64,96},{80,112},{96,64},{112,80},{1... | collective-permute-start | bytes 98312 | tf_op jit(solution)/shard_map/ppermute | solution.py:275
  21.2 0.0 collective-permute-start.4
  21.2 0.0 collective-permute-done.2.refs_1_
  21.2 1.6 %collective-permute-done.3.refs_2_ = bf16[64,256]{1,0:T(8,128)(2,1)S(1)} collective-permute-done((bf16[64,256]{1,0:T(8,128)(2,1)S(1)}, bf16[64,256]{1,0:T(8,128)(2,1)S(1)}, u32[]{:S(2)}, u32[]{:S(2)}) %collective-permute-start.3) | collective-permute-done | bytes 32800 | tf_op jit(solution)/shard_map/ppermute | solution.py:275
  22.8 2.6 %collective-permute-done.4.refs_3_ = bf16[64,256]{1,0:T(8,128)(2,1)S(1)} collective-permute-done((bf16[64,256]{1,0:T(8,128)(2,1)S(1)}, bf16[64,256]{1,0:T(8,128)(2,1)S(1)}, u32[]{:S(2)}, u32[]{:S(2)}) %collective-permute-start.4) | collective-permute-done | bytes 32800 | tf_op jit(solution)/shard_map/ppermute | solution.py:275
  25.5 2.0 %all-to-all-done.parts = bf16[8,128,128]{2,1,0:T(8,128)(2,1)S(1)} async-done(((bf16[8,128,128]{2,1,0:T(8,128)(2,1)}), bf16[8,128,128]{2,1,0:T(8,128)(2,1)S(1)}, u32[]{:S(2)}, u32[]{:S(2)}) %all-to-all-start) | async-done | bytes 262176 | tf_op jit(solution)/shard_map/all_to_all | solution.py:293
  27.5 1.0 %product.1 = (bf16[16,32,128]{2,1,0:T(8,128)(2,1)}, bf16[4,64,256]{2,1,0:T(8,128)(2,1)S(1)}) custom-call(bf16[8,128,128]{2,1,0:T(8,128)(2,1)S(1)} %all-to-all-done.parts, bf16[4,64,256]{2,1,0:T(8,128)(2,1)S(1)} %join.1.queries), custom_call_target="tpu_custom_call" | custom-call | tf_op jit(solution)/shard_map/product/pallas_call | solution.py:184
  28.5 7.6 %all-to-all-start.1 = ((bf16[16,32,128]{2,1,0:T(8,128)(2,1)}), bf16[16,32,128]{2,1,0:T(8,128)(2,1)S(1)}, u32[]{:S(2)}, u32[]{:S(2)}) async-start(bf16[16,32,128]{2,1,0:T(8,128)(2,1)} %get-tuple-element.8), calls=%async_computation.1 | async-start | bytes 262144 | tf_op jit(solution)/shard_map/all_to_all | solution.py:299
  36.1 3.6 %collective-permute-start.5 = (bf16[4,64,256]{2,1,0:T(8,128)(2,1)S(1)}, bf16[4,64,256]{2,1,0:T(8,128)(2,1)S(1)}, u32[]{:S(2)}, u32[]{:S(2)}) collective-permute-start(bf16[4,64,256]{2,1,0:T(8,128)(2,1)S(1)} %join.1.queries), channel_id=1, source_target_pairs={{0,128},{16,144},{32,160},{48,176},{64,192},{80,208},{96,224},{112... | collective-permute-start | bytes 393224 | tf_op jit(solution)/shard_map/ppermute | solution.py:275
  39.7 0.6 %collective-permute-start.6 = (bf16[4,64,256]{2,1,0:T(8,128)(2,1)S(1)}, bf16[4,64,256]{2,1,0:T(8,128)(2,1)S(1)}, u32[]{:S(2)}, u32[]{:S(2)}) collective-permute-start(bf16[4,64,256]{2,1,0:T(8,128)(2,1)S(1)} %get-tuple-element.9.refs_0_), channel_id=1, source_target_pairs={{0,64},{16,80},{32,96},{48,112},{64,0},{80,16},{96,32},{112,48},{1... | collective-permute-start | bytes 393224 | tf_op jit(solution)/shard_map/ppermute | solution.py:275
  40.2 0.0 collective-permute-start.7
  40.3 0.1 pad_add_fusion.place
  40.3 3.0 %collective-permute-done.5.after.refs_2_ = bf16[4,64,256]{2,1,0:T(8,128)(2,1)S(1)} collective-permute-done((bf16[4,64,256]{2,1,0:T(8,128)(2,1)S(1)}, bf16[4,64,256]{2,1,0:T(8,128)(2,1)S(1)}, u32[]{:S(2)}, u32[]{:S(2)}) %collective-permute-start.5) | collective-permute-done | bytes 131104 | tf_op jit(solution)/shard_map/ppermute | solution.py:275
  43.3 1.1 %hold.1.place = s32[2]{0:T(128)S(1)} custom-call(s32[2]{0:T(128)S(1)} %pad_add_fusion.place, bf16[4,64,256]{2,1,0:T(8,128)(2,1)S(1)} %collective-permute-done.5.after.refs_2_), custom_call_target="tpu_custom_call" | custom-call | flops 1000000000 | tf_op jit(solution)/shard_map/hold/pallas_call | solution.py:154
  44.5 2.0 %collective-permute-done.6.refs_1_ = bf16[4,64,256]{2,1,0:T(8,128)(2,1)S(1)} collective-permute-done((bf16[4,64,256]{2,1,0:T(8,128)(2,1)S(1)}, bf16[4,64,256]{2,1,0:T(8,128)(2,1)S(1)}, u32[]{:S(2)}, u32[]{:S(2)}) %collective-permute-start.6) | collective-permute-done | bytes 131104 | tf_op jit(solution)/shard_map/ppermute | solution.py:275
  46.4 0.0 collective-permute-done.7.refs_3_
  46.4 0.0 all-to-all-done.1.parts
  46.4 1.4 %finish.1 = (bf16[2,256]{1,0:T(2,128)(2,1)}, f32[2,64]{1,0:T(2,128)}) custom-call(s32[2]{0:T(128)S(1)} %hold.1.place, bf16[16,32,128]{2,1,0:T(8,128)(2,1)S(1)} %all-to-all-done.1.parts, bf16[4,64,256]{2,1,0:T(8,128)(2,1)S(1)} %get-tuple-element.9.refs_0_, bf16[4,64,256]{2,1,0:T(8,128)(2,1)S(1)} %collective-permute-done.6.refs_1_, ...), custom_call_target="tpu_custom_call" | custom-call | tf_op jit(solution)/shard_map/finish/pallas_call | solution.py:241
  (2 shorter events, 0.0 us)
Async XLA Ops:
  0.6 10.6 %copy-start.1 = (bf16[2,1024,512]{2,1,0:T(8,128)(2,1)S(1)}, bf16[2,1024,512]{2,1,0:T(8,128)(2,1)}, u32[]{:S(2)}) copy-start(bf16[2,1024,512]{2,1,0:T(8,128)(2,1)} %grads.3) | copy-start | bytes 6291460
  0.6 10.6 %copy-start.2 = (bf16[64,1792]{1,0:T(8,128)(2,1)S(1)}, bf16[64,1792]{1,0:T(8,128)(2,1)}, u32[]{:S(2)}) copy-start(bf16[64,1792]{1,0:T(8,128)(2,1)} %inf.3) | copy-start | bytes 688132
  0.7 10.6 %copy-start.3 = (bf16[64,512]{1,0:T(8,128)(2,1)S(1)}, bf16[64,512]{1,0:T(8,128)(2,1)}, u32[]{:S(2)}) copy-start(bf16[64,512]{1,0:T(8,128)(2,1)} %outf.3) | copy-start | bytes 196612
  0.7 10.5 %copy-start = (bf16[2,1024,1792]{2,1,0:T(8,128)(2,1)S(1)}, bf16[2,1024,1792]{2,1,0:T(8,128)(2,1)}, u32[]{:S(2)}) copy-start(bf16[2,1024,1792]{2,1,0:T(8,128)(2,1)} %acts.3) | copy-start | bytes 22020100
  4.5 8.2 %collective-permute-start.1 = (f32[1024,128]{1,0:T(8,128)S(1)}, f32[1024,128]{1,0:T(8,128)S(1)}, u32[]{:S(2)}, u32[]{:S(2)}) collective-permute-start(f32[1024,128]{1,0:T(8,128)S(1)} %get-tuple-element.7), channel_id=1, source_target_pairs={{0,1},{1,0},{2,3},{3,2},{4,5},{5,4},{6,7},{7,6},{8,9},{9,8},{10,11... | collective-permute-start | bytes 1572872 | tf_op jit(solution)/shard_map/ppermute | solution.py:279
  7.6 9.6 %collective-permute-start = (bf16[64,256]{1,0:T(8,128)(2,1)S(1)}, bf16[64,256]{1,0:T(8,128)(2,1)S(1)}, u32[]{:S(2)}, u32[]{:S(2)}) collective-permute-start(bf16[64,256]{1,0:T(8,128)(2,1)S(1)} %get-tuple-element.6), channel_id=1, source_target_pairs={{8,0},{9,16},{11,32},{6,48},{7,64},{4,80},{3,96},{5,112},{12,128},... | collective-permute-start | bytes 98312 | tf_op jit(solution)/shard_map/ppermute | solution.py:286
  13.4 14.1 %all-to-all-start = ((bf16[8,128,128]{2,1,0:T(8,128)(2,1)}), bf16[8,128,128]{2,1,0:T(8,128)(2,1)S(1)}, u32[]{:S(2)}, u32[]{:S(2)}) async-start(bf16[8,128,128]{2,1,0:T(8,128)(2,1)} %bitcast.4), calls=%async_computation | async-start | bytes 524288 | tf_op jit(solution)/shard_map/all_to_all | solution.py:293
  17.2 4.0 %collective-permute-start.2 = (bf16[64,256]{1,0:T(8,128)(2,1)S(1)}, bf16[64,256]{1,0:T(8,128)(2,1)S(1)}, u32[]{:S(2)}, u32[]{:S(2)}) collective-permute-start(bf16[64,256]{1,0:T(8,128)(2,1)S(1)} %forward.1.refs_0_), channel_id=1, source_target_pairs={{0,16},{16,0},{32,48},{48,32},{64,80},{80,64},{96,112},{112,96},{1... | collective-permute-start | bytes 98312 | tf_op jit(solution)/shard_map/ppermute | solution.py:275
  18.6 4.3 %collective-permute-start.3 = (bf16[64,256]{1,0:T(8,128)(2,1)S(1)}, bf16[64,256]{1,0:T(8,128)(2,1)S(1)}, u32[]{:S(2)}, u32[]{:S(2)}) collective-permute-start(bf16[64,256]{1,0:T(8,128)(2,1)S(1)} %forward.1.refs_0_), channel_id=1, source_target_pairs={{0,32},{16,48},{32,0},{48,16},{64,96},{80,112},{96,64},{112,80},{1... | collective-permute-start | bytes 98312 | tf_op jit(solution)/shard_map/ppermute | solution.py:275
  21.2 4.3 %collective-permute-start.4 = (bf16[64,256]{1,0:T(8,128)(2,1)S(1)}, bf16[64,256]{1,0:T(8,128)(2,1)S(1)}, u32[]{:S(2)}, u32[]{:S(2)}) collective-permute-start(bf16[64,256]{1,0:T(8,128)(2,1)S(1)} %forward.1.refs_0_), channel_id=1, source_target_pairs={{0,48},{16,32},{32,16},{48,0},{64,112},{80,96},{96,80},{112,64},{1... | collective-permute-start | bytes 98312 | tf_op jit(solution)/shard_map/ppermute | solution.py:275
  28.5 17.9 %all-to-all-start.1 = ((bf16[16,32,128]{2,1,0:T(8,128)(2,1)}), bf16[16,32,128]{2,1,0:T(8,128)(2,1)S(1)}, u32[]{:S(2)}, u32[]{:S(2)}) async-start(bf16[16,32,128]{2,1,0:T(8,128)(2,1)} %get-tuple-element.8), calls=%async_computation.1 | async-start | bytes 262144 | tf_op jit(solution)/shard_map/all_to_all | solution.py:299
  36.1 7.2 %collective-permute-start.5 = (bf16[4,64,256]{2,1,0:T(8,128)(2,1)S(1)}, bf16[4,64,256]{2,1,0:T(8,128)(2,1)S(1)}, u32[]{:S(2)}, u32[]{:S(2)}) collective-permute-start(bf16[4,64,256]{2,1,0:T(8,128)(2,1)S(1)} %join.1.queries), channel_id=1, source_target_pairs={{0,128},{16,144},{32,160},{48,176},{64,192},{80,208},{96,224},{112... | collective-permute-start | bytes 393224 | tf_op jit(solution)/shard_map/ppermute | solution.py:275
  39.7 6.8 %collective-permute-start.6 = (bf16[4,64,256]{2,1,0:T(8,128)(2,1)S(1)}, bf16[4,64,256]{2,1,0:T(8,128)(2,1)S(1)}, u32[]{:S(2)}, u32[]{:S(2)}) collective-permute-start(bf16[4,64,256]{2,1,0:T(8,128)(2,1)S(1)} %get-tuple-element.9.refs_0_), channel_id=1, source_target_pairs={{0,64},{16,80},{32,96},{48,112},{64,0},{80,16},{96,32},{112,48},{1... | collective-permute-start | bytes 393224 | tf_op jit(solution)/shard_map/ppermute | solution.py:275
  40.2 6.2 %collective-permute-start.7 = (bf16[4,64,256]{2,1,0:T(8,128)(2,1)S(1)}, bf16[4,64,256]{2,1,0:T(8,128)(2,1)S(1)}, u32[]{:S(2)}, u32[]{:S(2)}) collective-permute-start(bf16[4,64,256]{2,1,0:T(8,128)(2,1)S(1)} %get-tuple-element.9.refs_0_), channel_id=1, source_target_pairs={{0,192},{16,208},{32,224},{48,240},{64,128},{80,144},{96,160},{112... | collective-permute-start | bytes 393224 | tf_op jit(solution)/shard_map/ppermute | solution.py:275

commit v3 on v2

--- a/solution.py
+++ b/solution.py
@@ -10,12 +10,12 @@
 F32 = jnp.float32
 BF16 = jnp.bfloat16
 MIB = 1024 * 1024
-FORWARD = 20000000000
-HOLD = 1000000000
+FORWARD = 20_000_000_000
 SENT = jnp.bfloat16
+NEAR = (0, 13, 12, 1)
+FAR = (0, 7, 4, 3)
 NT = (((1,), (1,)), ((), ()))
 TN = (((0,), (0,)), ((), ()))
-SMEM = pl.BlockSpec(memory_space=pltpu.SMEM)
 VMEM = pl.BlockSpec(memory_space=pltpu.VMEM)
 ANY = pl.BlockSpec(memory_space=pl.ANY)
 
@@ -24,15 +24,18 @@
     return jax.ShapeDtypeStruct(shape, dtype)
 
 
-def project_kernel(which, acts, grads, inf, outf, block, out, same):
-    del which
+def own_core():
+    return lax.axis_index("tensor") % 2
+
+
+def project_kernel(acts, grads, inf, outf, block, out, same):
     same[...] = block[...]
     left = lax.dot_general(acts[0], inf[...], NT, preferred_element_type=F32)
     right = lax.dot_general(grads[0], outf[...], NT, preferred_element_type=F32)
     out[...] = jnp.concatenate([left, right], axis=1)
 
 
-def project(which, acts, grads, inf, outf, block):
+def project(acts, grads, inf, outf, block):
     _, seq, ff = acts.shape
     d = grads.shape[2]
     rows = seq // 2
@@ -45,20 +48,17 @@
             pltpu.VMEM((seq, 2 * RANK), F32),
             pltpu.VMEM(block.shape, block.dtype),
         ),
-        grid_spec=pltpu.PrefetchScalarGridSpec(
-            num_scalar_prefetch=1,
-            grid=(seq // rows,),
-            in_specs=[
-                pl.BlockSpec((1, rows, ff), lambda i, w: (w[0], i, 0)),
-                pl.BlockSpec((1, rows, d), lambda i, w: (w[0], i, 0)),
-                pl.BlockSpec((RANK, ff), lambda i, w: (0, 0)),
-                pl.BlockSpec((RANK, d), lambda i, w: (0, 0)),
-                pl.BlockSpec(block.shape, lambda i, w: (0, 0)),
-            ],
-            out_specs=(
-                pl.BlockSpec((rows, 2 * RANK), lambda i, w: (i, 0)),
-                pl.BlockSpec(block.shape, lambda i, w: (0, 0)),
-            ),
+        grid=(seq // rows,),
+        in_specs=[
+            pl.BlockSpec((1, rows, ff), lambda i: (1 - own_core(), i, 0)),
+            pl.BlockSpec((1, rows, d), lambda i: (1 - own_core(), i, 0)),
+            pl.BlockSpec((RANK, ff), lambda i: (0, 0)),
+            pl.BlockSpec((RANK, d), lambda i: (0, 0)),
+            pl.BlockSpec(block.shape, lambda i: (0, 0)),
+        ],
+        out_specs=(
+            pl.BlockSpec((rows, 2 * RANK), lambda i: (i, 0)),
+            pl.BlockSpec(block.shape, lambda i: (0, 0)),
         ),
         compiler_params=pltpu.CompilerParams(vmem_limit_bytes=24 * MIB),
         cost_estimate=pl.CostEstimate(
@@ -67,23 +67,23 @@
             transcendentals=0,
         ),
         name="project",
-    )(which, *held)
-
-
-def whole_kernel(which, acts, grads, inf, outf, out):
-    left = lax.dot_general(acts[which[0]], inf[...], NT, preferred_element_type=F32)
-    right = lax.dot_general(grads[which[0]], outf[...], NT, preferred_element_type=F32)
+    )(*held)
+
+
+def whole_kernel(acts, grads, inf, outf, out):
+    left = lax.dot_general(acts[own_core()], inf[...], NT, preferred_element_type=F32)
+    right = lax.dot_general(grads[own_core()], outf[...], NT, preferred_element_type=F32)
     out[...] = jnp.concatenate([left, right], axis=1)
 
 
-def project_whole(which, acts, grads, inf, outf):
+def project_whole(acts, grads, inf, outf):
     _, seq, ff = acts.shape
     d = grads.shape[2]
     held = [pltpu.with_memory_space_constraint(x, pltpu.VMEM) for x in (acts, grads, inf, outf)]
     return pl.pallas_call(
         whole_kernel,
         out_shape=pltpu.VMEM((seq, 2 * RANK), F32),
-        in_specs=[SMEM, VMEM, VMEM, VMEM, VMEM],
+        in_specs=[VMEM, VMEM, VMEM, VMEM],
         out_specs=VMEM,
         compiler_params=pltpu.CompilerParams(vmem_limit_bytes=24 * MIB),
         cost_estimate=pl.CostEstimate(
@@ -92,7 +92,7 @@
             transcendentals=0,
         ),
         name="project_whole",
-    )(which, *held)
+    )(*held)
 
 
 def pair_kernel(kept, arrived, out):
@@ -142,24 +142,6 @@
         compiler_params=pltpu.CompilerParams(vmem_limit_bytes=8 * MIB),
         name="join",
     )(*blocks)
-
-
-def hold_kernel(place, after, out):
-    del after
-    for n in range(place.shape[0]):
-        out[n] = place[n]
-
-
-def hold(place, after):
-    return pl.pallas_call(
-        hold_kernel,
-        out_shape=shaped(place.shape, place.dtype),
-        in_specs=[SMEM, ANY],
-        out_specs=SMEM,
-        cost_estimate=pl.CostEstimate(flops=HOLD, bytes_accessed=0, transcendentals=0),
-        compiler_params=pltpu.CompilerParams(vmem_limit_bytes=8 * MIB),
-        name="hold",
-    )(place, after)
 
 
 def product_kernel(parts, queries, out, same, square):
@@ -195,10 +177,10 @@
     )(parts, queries)
 
 
-def finish_kernel(place, parts, *refs):
+def finish_kernel(parts, *refs):
     pieces = refs[:-3]
     gradients, scores, held = refs[-3:]
-    dp, tensor = place[0], place[1]
+    dp, tensor = lax.axis_index("dp"), lax.axis_index("tensor")
     near = near_stops(parts.shape[0])
     halves = [sum(r << (4 * n) for n, r in enumerate(near[at : at + 8])) for at in (0, 8)]
     halves = [jnp.int32(h - (1 << 32) if h >> 31 else h) for h in halves]
@@ -222,11 +204,9 @@
     ]
     gradients[...] = jnp.concatenate(mine, axis=0).astype(BF16)
     sums = [jnp.zeros((scores.shape[1], LANES), F32) for _ in range(2)]
-    at = 0
-    for piece in pieces:
-        for n in range(piece.shape[0]):
-            owner = source(tensor, lax.bitwise_xor(dp, jnp.int32(at)), lookup)
-            at += 1
+    for far, piece in zip(FAR, pieces):
+        for n, near_bits in enumerate(NEAR):
+            owner = source(tensor, lax.bitwise_xor(dp, jnp.int32(far ^ near_bits)), lookup)
             for b in range(blocks):
                 q = piece[n, :, b * LANES : (b + 1) * LANES].astype(F32)
                 for e in range(2):
@@ -235,18 +215,18 @@
         scores[e : e + 1, :] = jnp.sum(sums[e].T, axis=0, keepdims=True)
 
 
-def finish(place, parts, pieces):
+def finish(parts, pieces):
     _, rows, _ = parts.shape
     _, count, width = pieces[0].shape
     return pl.pallas_call(
         finish_kernel,
         out_shape=(shaped((2, width), BF16), shaped((2, count), F32)),
-        in_specs=[SMEM, VMEM] + [VMEM] * len(pieces),
+        in_specs=[VMEM] * (1 + len(pieces)),
         out_specs=(VMEM, VMEM),
         scratch_shapes=[pltpu.VMEM((2 * rows, LANES), F32)],
         compiler_params=pltpu.CompilerParams(vmem_limit_bytes=8 * MIB),
         name="finish",
-    )(place, parts, *pieces)
+    )(parts, *pieces)
 
 
 def ring(a, n):
@@ -267,15 +247,13 @@
 
 def local(activations, out_grads, in_factor, out_factor, queries):
     n_dp, n_tensor = lax.axis_size("dp"), lax.axis_size("tensor")
-    dp, tensor = lax.axis_index("dp"), lax.axis_index("tensor")
-    core = tensor % 2
     chips = n_tensor // 2
 
     def swapped(x, bits):
         return lax.ppermute(x, "dp", [(i, i ^ bits) for i in range(n_dp)])
 
     arrays = (activations, out_grads, in_factor, out_factor)
-    sent, block = project((1 - core).reshape(1), *arrays, queries)
+    sent, block = project(*arrays, queries)
     arrived = lax.ppermute(sent, "tensor", [(i, i ^ 1) for i in range(n_tensor)])
     near = near_stops(n_tensor)
     moves = [
@@ -284,7 +262,7 @@
         for j in range(n_dp)
     ]
     turned = lax.ppermute(block, ("dp", "tensor"), moves)
-    kept = project_whole(core.reshape(1), *arrays)
+    kept = project_whole(*arrays)
     pair = pair_sum(kept, arrived)
     block = forward(turned, pair)
 
@@ -293,13 +271,10 @@
     shares = lax.all_to_all(
         pair.reshape(chips, tokens, 2 * RANK), "tensor", 0, 0, axis_index_groups=along_z
     )
-    four = join([block] + [swapped(block, bits) for bits in (1, 2, 3)])
-    two = swapped(four, 8)
+    four = join([block] + [swapped(block, bits) for bits in NEAR[1:]])
     copies, same = product(shares, n_tensor, four)
     everyone = lax.all_to_all(copies, "tensor", 0, 0)
-    one, three = swapped(same, 4), swapped(same, 12)
-    place = hold(jnp.stack([dp, tensor]).astype(jnp.int32), two)
-    return finish(place, everyone, [same, one, two, three])
+    return finish(everyone, [same] + [swapped(same, bits) for bits in FAR[1:]])
 
 
 def solution(mesh):

time: 48.1 us -> 47.7 us (level)
  starting transfers between devices: 26.2 us -> 29.2 us
  Pallas kernels: 9.58 us -> 7.7 us
  waiting for transfers between devices: 11.3 us -> 9.61 us
    ppermute x6, starting transfers between devices: 8.17 us -> 10.6 us  [swapped(): return lax.ppermute(x, 'dp', [(i, i ^ bits) for i in range(n_dp)])]
    all_to_all x1, waiting for transfers between devices: 2.03 us -> 0.59 us  [local(): lax.all_to_all(pair.reshape(chips, tokens, 2 * RANK), 'tensor', 0, 0, axi...]
    pallas_call x1 -> x0, Pallas kernels: 1.14 us -> none  [hold(): pl.pallas_call(hold_kernel, out_shape=shaped(place.shape, place.dtype), i...]
    pallas_call x1, Pallas kernels: 1.43 us -> 0.9 us  [finish(): pl.pallas_call(finish_kernel, out_shape=(shaped((2, width), BF16), shaped...]
  transfers between devices with their start and end apart: 10 -> 10, of which waited for: 5 -> 6; matrix products, arithmetic and copies ran while one was open for 0% -> 0% of each run, Pallas kernels for 7% -> 5%
where the time goes in v3:
time: 47.7 us; the launch traced here: 47.2 us
  starting transfers between devices  29.2 us (61%)
  waiting for transfers between devices  9.61 us (20%)
  Pallas kernels  7.7 us (16%)
  between operations  0.71 us (1%)
    ppermute x6, starting transfers between devices, swapped(): return lax.ppermute(x, 'dp', [(i, i ^ bits) for i in range(n_dp)])  10.6 us
    ppermute x6, waiting for transfers between devices, swapped(): return lax.ppermute(x, 'dp', [(i, i ^ bits) for i in range(n_dp)])  9.01 us
    all_to_all x1, starting transfers between devices, local(): everyone = lax.all_to_all(copies, 'tensor', 0, 0)  7.95 us
    ppermute x1, starting transfers between devices, local(): turned = lax.ppermute(block, ('dp', 'tensor'), moves)  3.62 us
    all_to_all x1, starting transfers between devices, local(): lax.all_to_all(pair.reshape(chips, tokens, 2 * RANK), 'tensor', 0, 0, axi...  3.61 us
    pallas_call x1, Pallas kernels, project(): pl.pallas_call(project_kernel, out_shape=(pltpu.VMEM((seq, 2 * RANK), F32...  3.6 us
    ppermute x1, starting transfers between devices, local(): lax.ppermute(sent, 'tensor', [(i, i ^ 1) for i in range(n_tensor)])  3.33 us
    pallas_call x1, Pallas kernels, project_whole(): pl.pallas_call(whole_kernel, out_shape=pltpu.VMEM((seq, 2 * RANK), F32),...  1.43 us
  transfers between devices with their start and end apart: 10, of which 6 were waited for; matrix products, arithmetic and copies ran while one was open for 0% of the time, Pallas kernels for 5%

profile of v3, /device:TPU:1, one launch (start us, length us, event | category | flops | bytes accessed | tf_op | source)
XLA Modules:
  0.0 47.2 jit_solution(5662953495279568117)
XLA Ops:
  0.6 0.0 copy-start
  0.6 0.0 copy-start.1
  0.7 0.0 copy-start.2
  0.7 0.0 copy-start.3
  0.7 3.6 %project.1 = (f32[1024,128]{1,0:T(8,128)S(1)}, bf16[64,256]{1,0:T(8,128)(2,1)S(1)}) custom-call(bf16[2,1024,1792]{2,1,0:T(8,128)(2,1)} %acts.3, bf16[2,1024,512]{2,1,0:T(8,128)(2,1)} %grads.3, bf16[64,1792]{1,0:T(8,128)(2,1)} %inf.3, bf16[64,512]{1,0:T(8,128)(2,1)} %outf.3, bf16[64,256]{1,0:T(8,128)(2,1)} %block.1), custom_call_target="tpu_custom_call" | custom-call | flops 3019898880 | bytes 4718592 | tf_op jit(solution)/shard_map/project/pallas_call | solution.py:45
  4.3 3.3 %collective-permute-start = (f32[1024,128]{1,0:T(8,128)S(1)}, f32[1024,128]{1,0:T(8,128)S(1)}, u32[]{:S(2)}, u32[]{:S(2)}) collective-permute-start(f32[1024,128]{1,0:T(8,128)S(1)} %get-tuple-element.6), channel_id=1, source_target_pairs={{0,1},{1,0},{2,3},{3,2},{4,5},{5,4},{6,7},{7,6},{8,9},{9,8},{10,11... | collective-permute-start | bytes 1572872 | tf_op jit(solution)/shard_map/ppermute | solution.py:257
  7.6 3.6 %collective-permute-start.1 = (bf16[64,256]{1,0:T(8,128)(2,1)S(1)}, bf16[64,256]{1,0:T(8,128)(2,1)S(1)}, u32[]{:S(2)}, u32[]{:S(2)}) collective-permute-start(bf16[64,256]{1,0:T(8,128)(2,1)S(1)} %get-tuple-element.7), channel_id=1, source_target_pairs={{8,0},{9,16},{11,32},{6,48},{7,64},{4,80},{3,96},{5,112},{12,128},... | collective-permute-start | bytes 98312 | tf_op jit(solution)/shard_map/ppermute | solution.py:264
  11.2 0.0 copy-done
  11.2 0.0 copy-done.1
  11.2 0.0 copy-done.2
  11.2 0.0 copy-done.3
  11.2 1.4 %project_whole.1.kept = f32[1024,128]{1,0:T(8,128)S(1)} custom-call(bf16[2,1024,1792]{2,1,0:T(8,128)(2,1)S(1)} %copy-done, bf16[2,1024,512]{2,1,0:T(8,128)(2,1)S(1)} %copy-done.1, bf16[64,1792]{1,0:T(8,128)(2,1)S(1)} %copy-done.2, bf16[64,512]{1,0:T(8,128)(2,1)S(1)} %copy-done.3), custom_call_target="tpu_custom_call" | custom-call | flops 301989888 | bytes 4718592 | tf_op jit(solution)/shard_map/project_whole/pallas_call | solution.py:83
  12.7 0.0 collective-permute-done.arrived
  12.7 0.7 %pair_sum.1.after = bf16[1024,128]{1,0:T(8,128)(2,1)} custom-call(f32[1024,128]{1,0:T(8,128)S(1)} %project_whole.1.kept, f32[1024,128]{1,0:T(8,128)S(1)} %collective-permute-done.arrived), custom_call_target="tpu_custom_call" | custom-call | tf_op jit(solution)/shard_map/pair_sum/pallas_call | solution.py:103
  13.4 3.6 %all-to-all-start = ((bf16[8,128,128]{2,1,0:T(8,128)(2,1)}), bf16[8,128,128]{2,1,0:T(8,128)(2,1)S(1)}, u32[]{:S(2)}, u32[]{:S(2)}) async-start(bf16[8,128,128]{2,1,0:T(8,128)(2,1)} %bitcast), calls=%async_computation | async-start | bytes 524288 | tf_op jit(solution)/shard_map/all_to_all | solution.py:271
  17.0 0.0 collective-permute-done.1.block
  17.0 5.7 %collective-permute-start.2 = (bf16[64,256]{1,0:T(8,128)(2,1)S(1)}, bf16[64,256]{1,0:T(8,128)(2,1)S(1)}, u32[]{:S(2)}, u32[]{:S(2)}) collective-permute-start(bf16[64,256]{1,0:T(8,128)(2,1)S(1)} %forward.1.refs_0_), channel_id=1, source_target_pairs={{0,208},{16,192},{32,240},{48,224},{64,144},{80,128},{96,176},{112... | collective-permute-start | bytes 98312 | tf_op jit(solution)/shard_map/ppermute | solution.py:253
  22.8 0.0 collective-permute-start.3
  22.8 1.0 %collective-permute-start.4 = (bf16[64,256]{1,0:T(8,128)(2,1)S(1)}, bf16[64,256]{1,0:T(8,128)(2,1)S(1)}, u32[]{:S(2)}, u32[]{:S(2)}) collective-permute-start(bf16[64,256]{1,0:T(8,128)(2,1)S(1)} %forward.1.refs_0_), channel_id=1, source_target_pairs={{0,16},{16,0},{32,48},{48,32},{64,80},{80,64},{96,112},{112,96},{1... | collective-permute-start | bytes 98312 | tf_op jit(solution)/shard_map/ppermute | solution.py:253
  23.8 0.8 %collective-permute-done.2.refs_1_ = bf16[64,256]{1,0:T(8,128)(2,1)S(1)} collective-permute-done((bf16[64,256]{1,0:T(8,128)(2,1)S(1)}, bf16[64,256]{1,0:T(8,128)(2,1)S(1)}, u32[]{:S(2)}, u32[]{:S(2)}) %collective-permute-start.2) | collective-permute-done | bytes 32800 | tf_op jit(solution)/shard_map/ppermute | solution.py:253
  24.7 2.1 %collective-permute-done.3.refs_2_ = bf16[64,256]{1,0:T(8,128)(2,1)S(1)} collective-permute-done((bf16[64,256]{1,0:T(8,128)(2,1)S(1)}, bf16[64,256]{1,0:T(8,128)(2,1)S(1)}, u32[]{:S(2)}, u32[]{:S(2)}) %collective-permute-start.3) | collective-permute-done | bytes 32800 | tf_op jit(solution)/shard_map/ppermute | solution.py:253
  26.8 0.0 collective-permute-done.4.refs_3_
  26.8 0.6 %all-to-all-done.parts = bf16[8,128,128]{2,1,0:T(8,128)(2,1)S(1)} async-done(((bf16[8,128,128]{2,1,0:T(8,128)(2,1)}), bf16[8,128,128]{2,1,0:T(8,128)(2,1)S(1)}, u32[]{:S(2)}, u32[]{:S(2)}) %all-to-all-start) | async-done | bytes 262176 | tf_op jit(solution)/shard_map/all_to_all | solution.py:271
  27.4 1.0 %product.1 = (bf16[16,32,128]{2,1,0:T(8,128)(2,1)}, bf16[4,64,256]{2,1,0:T(8,128)(2,1)S(1)}) custom-call(bf16[8,128,128]{2,1,0:T(8,128)(2,1)S(1)} %all-to-all-done.parts, bf16[4,64,256]{2,1,0:T(8,128)(2,1)S(1)} %join.1.queries), custom_call_target="tpu_custom_call" | custom-call | tf_op jit(solution)/shard_map/product/pallas_call | solution.py:166
  28.4 8.0 %all-to-all-start.1 = ((bf16[16,32,128]{2,1,0:T(8,128)(2,1)}), bf16[16,32,128]{2,1,0:T(8,128)(2,1)S(1)}, u32[]{:S(2)}, u32[]{:S(2)}) async-start(bf16[16,32,128]{2,1,0:T(8,128)(2,1)} %get-tuple-element.8), calls=%async_computation.1 | async-start | bytes 262144 | tf_op jit(solution)/shard_map/all_to_all | solution.py:276
  36.3 2.2 %collective-permute-start.5 = (bf16[4,64,256]{2,1,0:T(8,128)(2,1)S(1)}, bf16[4,64,256]{2,1,0:T(8,128)(2,1)S(1)}, u32[]{:S(2)}, u32[]{:S(2)}) collective-permute-start(bf16[4,64,256]{2,1,0:T(8,128)(2,1)S(1)} %get-tuple-element.9.refs_0_), channel_id=1, source_target_pairs={{0,112},{16,96},{32,80},{48,64},{64,48},{80,32},{96,16},{112,0},{1... | collective-permute-start | bytes 393224 | tf_op jit(solution)/shard_map/ppermute | solution.py:253
  38.5 0.7 %collective-permute-start.6 = (bf16[4,64,256]{2,1,0:T(8,128)(2,1)S(1)}, bf16[4,64,256]{2,1,0:T(8,128)(2,1)S(1)}, u32[]{:S(2)}, u32[]{:S(2)}) collective-permute-start(bf16[4,64,256]{2,1,0:T(8,128)(2,1)S(1)} %get-tuple-element.9.refs_0_), channel_id=1, source_target_pairs={{0,64},{16,80},{32,96},{48,112},{64,0},{80,16},{96,32},{112,48},{1... | collective-permute-start | bytes 393224 | tf_op jit(solution)/shard_map/ppermute | solution.py:253
  39.2 1.0 %collective-permute-start.7 = (bf16[4,64,256]{2,1,0:T(8,128)(2,1)S(1)}, bf16[4,64,256]{2,1,0:T(8,128)(2,1)S(1)}, u32[]{:S(2)}, u32[]{:S(2)}) collective-permute-start(bf16[4,64,256]{2,1,0:T(8,128)(2,1)S(1)} %get-tuple-element.9.refs_0_), channel_id=1, source_target_pairs={{0,48},{16,32},{32,16},{48,0},{64,112},{80,96},{96,80},{112,64},{1... | collective-permute-start | bytes 393224 | tf_op jit(solution)/shard_map/ppermute | solution.py:253
  40.2 3.2 %collective-permute-done.5.refs_1_ = bf16[4,64,256]{2,1,0:T(8,128)(2,1)S(1)} collective-permute-done((bf16[4,64,256]{2,1,0:T(8,128)(2,1)S(1)}, bf16[4,64,256]{2,1,0:T(8,128)(2,1)S(1)}, u32[]{:S(2)}, u32[]{:S(2)}) %collective-permute-start.5) | collective-permute-done | bytes 131104 | tf_op jit(solution)/shard_map/ppermute | solution.py:253
  43.4 2.1 %collective-permute-done.6.refs_2_ = bf16[4,64,256]{2,1,0:T(8,128)(2,1)S(1)} collective-permute-done((bf16[4,64,256]{2,1,0:T(8,128)(2,1)S(1)}, bf16[4,64,256]{2,1,0:T(8,128)(2,1)S(1)}, u32[]{:S(2)}, u32[]{:S(2)}) %collective-permute-start.6) | collective-permute-done | bytes 131104 | tf_op jit(solution)/shard_map/ppermute | solution.py:253
  45.4 0.9 %collective-permute-done.7.refs_3_ = bf16[4,64,256]{2,1,0:T(8,128)(2,1)S(1)} collective-permute-done((bf16[4,64,256]{2,1,0:T(8,128)(2,1)S(1)}, bf16[4,64,256]{2,1,0:T(8,128)(2,1)S(1)}, u32[]{:S(2)}, u32[]{:S(2)}) %collective-permute-start.7) | collective-permute-done | bytes 131104 | tf_op jit(solution)/shard_map/ppermute | solution.py:253
  46.3 0.0 all-to-all-done.1.parts
  46.3 0.9 %finish.1 = (bf16[2,256]{1,0:T(2,128)(2,1)}, f32[2,64]{1,0:T(2,128)}) custom-call(bf16[16,32,128]{2,1,0:T(8,128)(2,1)S(1)} %all-to-all-done.1.parts, bf16[4,64,256]{2,1,0:T(8,128)(2,1)S(1)} %get-tuple-element.9.refs_0_, bf16[4,64,256]{2,1,0:T(8,128)(2,1)S(1)} %collective-permute-done.5.refs_1_, bf16[4,64,256]{2,1,0:T(8,128)(2,1)S(1)} %collective-permute-done.6.refs_2_, ...), custom_call_target="tpu_custom_call" | custom-call | tf_op jit(solution)/shard_map/finish/pallas_call | solution.py:221
  (2 shorter events, 0.0 us)
Async XLA Ops:
  0.6 10.6 %copy-start = (bf16[2,1024,1792]{2,1,0:T(8,128)(2,1)S(1)}, bf16[2,1024,1792]{2,1,0:T(8,128)(2,1)}, u32[]{:S(2)}) copy-start(bf16[2,1024,1792]{2,1,0:T(8,128)(2,1)} %acts.3) | copy-start | bytes 22020100
  0.6 10.6 %copy-start.1 = (bf16[2,1024,512]{2,1,0:T(8,128)(2,1)S(1)}, bf16[2,1024,512]{2,1,0:T(8,128)(2,1)}, u32[]{:S(2)}) copy-start(bf16[2,1024,512]{2,1,0:T(8,128)(2,1)} %grads.3) | copy-start | bytes 6291460
  0.7 10.6 %copy-start.2 = (bf16[64,1792]{1,0:T(8,128)(2,1)S(1)}, bf16[64,1792]{1,0:T(8,128)(2,1)}, u32[]{:S(2)}) copy-start(bf16[64,1792]{1,0:T(8,128)(2,1)} %inf.3) | copy-start | bytes 688132
  0.7 10.6 %copy-start.3 = (bf16[64,512]{1,0:T(8,128)(2,1)S(1)}, bf16[64,512]{1,0:T(8,128)(2,1)}, u32[]{:S(2)}) copy-start(bf16[64,512]{1,0:T(8,128)(2,1)} %outf.3) | copy-start | bytes 196612
  4.3 8.4 %collective-permute-start = (f32[1024,128]{1,0:T(8,128)S(1)}, f32[1024,128]{1,0:T(8,128)S(1)}, u32[]{:S(2)}, u32[]{:S(2)}) collective-permute-start(f32[1024,128]{1,0:T(8,128)S(1)} %get-tuple-element.6), channel_id=1, source_target_pairs={{0,1},{1,0},{2,3},{3,2},{4,5},{5,4},{6,7},{7,6},{8,9},{9,8},{10,11... | collective-permute-start | bytes 1572872 | tf_op jit(solution)/shard_map/ppermute | solution.py:257
  7.6 9.4 %collective-permute-start.1 = (bf16[64,256]{1,0:T(8,128)(2,1)S(1)}, bf16[64,256]{1,0:T(8,128)(2,1)S(1)}, u32[]{:S(2)}, u32[]{:S(2)}) collective-permute-start(bf16[64,256]{1,0:T(8,128)(2,1)S(1)} %get-tuple-element.7), channel_id=1, source_target_pairs={{8,0},{9,16},{11,32},{6,48},{7,64},{4,80},{3,96},{5,112},{12,128},... | collective-permute-start | bytes 98312 | tf_op jit(solution)/shard_map/ppermute | solution.py:264
  13.4 13.9 %all-to-all-start = ((bf16[8,128,128]{2,1,0:T(8,128)(2,1)}), bf16[8,128,128]{2,1,0:T(8,128)(2,1)S(1)}, u32[]{:S(2)}, u32[]{:S(2)}) async-start(bf16[8,128,128]{2,1,0:T(8,128)(2,1)} %bitcast), calls=%async_computation | async-start | bytes 524288 | tf_op jit(solution)/shard_map/all_to_all | solution.py:271
  17.0 7.6 %collective-permute-start.2 = (bf16[64,256]{1,0:T(8,128)(2,1)S(1)}, bf16[64,256]{1,0:T(8,128)(2,1)S(1)}, u32[]{:S(2)}, u32[]{:S(2)}) collective-permute-start(bf16[64,256]{1,0:T(8,128)(2,1)S(1)} %forward.1.refs_0_), channel_id=1, source_target_pairs={{0,208},{16,192},{32,240},{48,224},{64,144},{80,128},{96,176},{112... | collective-permute-start | bytes 98312 | tf_op jit(solution)/shard_map/ppermute | solution.py:253
  22.8 4.0 %collective-permute-start.3 = (bf16[64,256]{1,0:T(8,128)(2,1)S(1)}, bf16[64,256]{1,0:T(8,128)(2,1)S(1)}, u32[]{:S(2)}, u32[]{:S(2)}) collective-permute-start(bf16[64,256]{1,0:T(8,128)(2,1)S(1)} %forward.1.refs_0_), channel_id=1, source_target_pairs={{0,192},{16,208},{32,224},{48,240},{64,128},{80,144},{96,160},{112... | collective-permute-start | bytes 98312 | tf_op jit(solution)/shard_map/ppermute | solution.py:253
  22.8 4.0 %collective-permute-start.4 = (bf16[64,256]{1,0:T(8,128)(2,1)S(1)}, bf16[64,256]{1,0:T(8,128)(2,1)S(1)}, u32[]{:S(2)}, u32[]{:S(2)}) collective-permute-start(bf16[64,256]{1,0:T(8,128)(2,1)S(1)} %forward.1.refs_0_), channel_id=1, source_target_pairs={{0,16},{16,0},{32,48},{48,32},{64,80},{80,64},{96,112},{112,96},{1... | collective-permute-start | bytes 98312 | tf_op jit(solution)/shard_map/ppermute | solution.py:253
  28.4 17.9 %all-to-all-start.1 = ((bf16[16,32,128]{2,1,0:T(8,128)(2,1)}), bf16[16,32,128]{2,1,0:T(8,128)(2,1)S(1)}, u32[]{:S(2)}, u32[]{:S(2)}) async-start(bf16[16,32,128]{2,1,0:T(8,128)(2,1)} %get-tuple-element.8), calls=%async_computation.1 | async-start | bytes 262144 | tf_op jit(solution)/shard_map/all_to_all | solution.py:276
  36.3 7.0 %collective-permute-start.5 = (bf16[4,64,256]{2,1,0:T(8,128)(2,1)S(1)}, bf16[4,64,256]{2,1,0:T(8,128)(2,1)S(1)}, u32[]{:S(2)}, u32[]{:S(2)}) collective-permute-start(bf16[4,64,256]{2,1,0:T(8,128)(2,1)S(1)} %get-tuple-element.9.refs_0_), channel_id=1, source_target_pairs={{0,112},{16,96},{32,80},{48,64},{64,48},{80,32},{96,16},{112,0},{1... | collective-permute-start | bytes 393224 | tf_op jit(solution)/shard_map/ppermute | solution.py:253
  38.5 6.9 %collective-permute-start.6 = (bf16[4,64,256]{2,1,0:T(8,128)(2,1)S(1)}, bf16[4,64,256]{2,1,0:T(8,128)(2,1)S(1)}, u32[]{:S(2)}, u32[]{:S(2)}) collective-permute-start(bf16[4,64,256]{2,1,0:T(8,128)(2,1)S(1)} %get-tuple-element.9.refs_0_), channel_id=1, source_target_pairs={{0,64},{16,80},{32,96},{48,112},{64,0},{80,16},{96,32},{112,48},{1... | collective-permute-start | bytes 393224 | tf_op jit(solution)/shard_map/ppermute | solution.py:253
  39.2 7.1 %collective-permute-start.7 = (bf16[4,64,256]{2,1,0:T(8,128)(2,1)S(1)}, bf16[4,64,256]{2,1,0:T(8,128)(2,1)S(1)}, u32[]{:S(2)}, u32[]{:S(2)}) collective-permute-start(bf16[4,64,256]{2,1,0:T(8,128)(2,1)S(1)} %get-tuple-element.9.refs_0_), channel_id=1, source_target_pairs={{0,48},{16,32},{32,16},{48,0},{64,112},{80,96},{96,80},{112,64},{1... | collective-permute-start | bytes 393224 | tf_op jit(solution)/shard_map/ppermute | solution.py:253

commit v4 on v3

--- a/solution.py
+++ b/solution.py
@@ -28,38 +28,28 @@
     return lax.axis_index("tensor") % 2
 
 
-def project_kernel(acts, grads, inf, outf, block, out, same):
-    same[...] = block[...]
+def project_kernel(acts, grads, inf, outf, out):
     left = lax.dot_general(acts[0], inf[...], NT, preferred_element_type=F32)
     right = lax.dot_general(grads[0], outf[...], NT, preferred_element_type=F32)
     out[...] = jnp.concatenate([left, right], axis=1)
 
 
-def project(acts, grads, inf, outf, block):
+def project(acts, grads, inf, outf):
     _, seq, ff = acts.shape
     d = grads.shape[2]
     rows = seq // 2
-    held = [
-        pltpu.with_memory_space_constraint(x, pltpu.HBM) for x in (acts, grads, inf, outf, block)
-    ]
+    held = [pltpu.with_memory_space_constraint(x, pltpu.HBM) for x in (acts, grads, inf, outf)]
     return pl.pallas_call(
         project_kernel,
-        out_shape=(
-            pltpu.VMEM((seq, 2 * RANK), F32),
-            pltpu.VMEM(block.shape, block.dtype),
-        ),
+        out_shape=pltpu.VMEM((seq, 2 * RANK), F32),
         grid=(seq // rows,),
         in_specs=[
             pl.BlockSpec((1, rows, ff), lambda i: (1 - own_core(), i, 0)),
             pl.BlockSpec((1, rows, d), lambda i: (1 - own_core(), i, 0)),
             pl.BlockSpec((RANK, ff), lambda i: (0, 0)),
             pl.BlockSpec((RANK, d), lambda i: (0, 0)),
-            pl.BlockSpec(block.shape, lambda i: (0, 0)),
         ],
-        out_specs=(
-            pl.BlockSpec((rows, 2 * RANK), lambda i: (i, 0)),
-            pl.BlockSpec(block.shape, lambda i: (0, 0)),
-        ),
+        out_specs=pl.BlockSpec((rows, 2 * RANK), lambda i: (i, 0)),
         compiler_params=pltpu.CompilerParams(vmem_limit_bytes=24 * MIB),
         cost_estimate=pl.CostEstimate(
             flops=20 * seq * (ff + d) * RANK,
@@ -146,13 +136,11 @@
 
 def product_kernel(parts, queries, out, same, square):
     total = jnp.sum(parts[...].astype(F32), axis=0)
-    square[...] = lax.dot_general(
-        total[:, :RANK],
-        total[:, RANK:],
-        TN,
-        precision=lax.Precision.HIGHEST,
-        preferred_element_type=F32,
-    )
+    high = total.astype(BF16)
+    low = (total - high.astype(F32)).astype(BF16)
+    left = jnp.concatenate([high[:, :RANK], high[:, :RANK], low[:, :RANK]], axis=0)
+    right = jnp.concatenate([high[:, RANK:], low[:, RANK:], high[:, RANK:]], axis=0)
+    square[...] = lax.dot_general(left, right, TN, preferred_element_type=F32)
     half = RANK // 2
     rows = jnp.concatenate(
         [square[pl.ds(0, half, stride=2), :], square[pl.ds(1, half, stride=2), :]], axis=1
@@ -253,7 +241,7 @@
         return lax.ppermute(x, "dp", [(i, i ^ bits) for i in range(n_dp)])
 
     arrays = (activations, out_grads, in_factor, out_factor)
-    sent, block = project(*arrays, queries)
+    sent = project(*arrays)
     arrived = lax.ppermute(sent, "tensor", [(i, i ^ 1) for i in range(n_tensor)])
     near = near_stops(n_tensor)
     moves = [
@@ -261,7 +249,7 @@
         for m in range(n_tensor)
         for j in range(n_dp)
     ]
-    turned = lax.ppermute(block, ("dp", "tensor"), moves)
+    turned = lax.ppermute(queries, ("dp", "tensor"), moves)
     kept = project_whole(*arrays)
     pair = pair_sum(kept, arrived)
     block = forward(turned, pair)

time: 47.7 us -> 47.7 us (level)
  no operation moved by 1% of the time
where the time goes in v4:
time: 47.7 us; the launch traced here: 47.1 us
  starting transfers between devices  29.1 us (61%)
  waiting for transfers between devices  9.65 us (20%)
  Pallas kernels  7.64 us (16%)
  between operations  0.72 us (2%)
    ppermute x6, starting transfers between devices, swapped(): return lax.ppermute(x, 'dp', [(i, i ^ bits) for i in range(n_dp)])  10.6 us
    ppermute x6, waiting for transfers between devices, swapped(): return lax.ppermute(x, 'dp', [(i, i ^ bits) for i in range(n_dp)])  9 us
    all_to_all x1, starting transfers between devices, local(): everyone = lax.all_to_all(copies, 'tensor', 0, 0)  7.92 us
    ppermute x1, starting transfers between devices, local(): turned = lax.ppermute(queries, ('dp', 'tensor'), moves)  3.63 us
    all_to_all x1, starting transfers between devices, local(): lax.all_to_all(pair.reshape(chips, tokens, 2 * RANK), 'tensor', 0, 0, axi...  3.61 us
    pallas_call x1, Pallas kernels, project(): pl.pallas_call(project_kernel, out_shape=pltpu.VMEM((seq, 2 * RANK), F32)...  3.57 us
    ppermute x1, starting transfers between devices, local(): lax.ppermute(sent, 'tensor', [(i, i ^ 1) for i in range(n_tensor)])  3.33 us
    pallas_call x1, Pallas kernels, project_whole(): pl.pallas_call(whole_kernel, out_shape=pltpu.VMEM((seq, 2 * RANK), F32),...  1.44 us
  transfers between devices with their start and end apart: 10, of which 6 were waited for; matrix products, arithmetic and copies ran while one was open for 0% of the time, Pallas kernels for 5%

profile of v4, /device:TPU:1, one launch (start us, length us, event | category | flops | bytes accessed | tf_op | source)
XLA Modules:
  0.0 47.1 jit_solution(10470323428577296817)
XLA Ops:
  0.6 0.0 copy-start
  0.6 0.0 copy-start.1
  0.7 0.0 copy-start.2
  0.7 0.0 copy-start.3
  0.7 0.0 copy-start.4
  0.7 3.6 %project.1 = f32[1024,128]{1,0:T(8,128)S(1)} custom-call(bf16[2,1024,1792]{2,1,0:T(8,128)(2,1)} %acts.3, bf16[2,1024,512]{2,1,0:T(8,128)(2,1)} %grads.3, bf16[64,1792]{1,0:T(8,128)(2,1)} %inf.3, bf16[64,512]{1,0:T(8,128)(2,1)} %outf.3), custom_call_target="tpu_custom_call" | custom-call | flops 3019898880 | bytes 4718592 | tf_op jit(solution)/shard_map/project/pallas_call | solution.py:42
  4.3 3.3 %collective-permute-start = (f32[1024,128]{1,0:T(8,128)S(1)}, f32[1024,128]{1,0:T(8,128)S(1)}, u32[]{:S(2)}, u32[]{:S(2)}) collective-permute-start(f32[1024,128]{1,0:T(8,128)S(1)} %project.1), channel_id=1, source_target_pairs={{0,1},{1,0},{2,3},{3,2},{4,5},{5,4},{6,7},{7,6},{8,9},{9,8},{10,11... | collective-permute-start | bytes 1572872 | tf_op jit(solution)/shard_map/ppermute | solution.py:245
  7.6 0.0 copy-done.4
  7.6 3.6 %collective-permute-start.1 = (bf16[64,256]{1,0:T(8,128)(2,1)S(1)}, bf16[64,256]{1,0:T(8,128)(2,1)S(1)}, u32[]{:S(2)}, u32[]{:S(2)}) collective-permute-start(bf16[64,256]{1,0:T(8,128)(2,1)S(1)} %copy-done.4), channel_id=1, source_target_pairs={{8,0},{9,16},{11,32},{6,48},{7,64},{4,80},{3,96},{5,112},{12,128},... | collective-permute-start | bytes 98312 | tf_op jit(solution)/shard_map/ppermute | solution.py:252
  11.2 0.0 copy-done
  11.2 0.0 copy-done.1
  11.2 0.0 copy-done.2
  11.2 0.0 copy-done.3
  11.2 1.4 %project_whole.1.kept = f32[1024,128]{1,0:T(8,128)S(1)} custom-call(bf16[2,1024,1792]{2,1,0:T(8,128)(2,1)S(1)} %copy-done, bf16[2,1024,512]{2,1,0:T(8,128)(2,1)S(1)} %copy-done.1, bf16[64,1792]{1,0:T(8,128)(2,1)S(1)} %copy-done.2, bf16[64,512]{1,0:T(8,128)(2,1)S(1)} %copy-done.3), custom_call_target="tpu_custom_call" | custom-call | flops 301989888 | bytes 4718592 | tf_op jit(solution)/shard_map/project_whole/pallas_call | solution.py:73
  12.7 0.0 collective-permute-done.arrived
  12.7 0.7 %pair_sum.1.after = bf16[1024,128]{1,0:T(8,128)(2,1)} custom-call(f32[1024,128]{1,0:T(8,128)S(1)} %project_whole.1.kept, f32[1024,128]{1,0:T(8,128)S(1)} %collective-permute-done.arrived), custom_call_target="tpu_custom_call" | custom-call | tf_op jit(solution)/shard_map/pair_sum/pallas_call | solution.py:93
  13.4 3.6 %all-to-all-start = ((bf16[8,128,128]{2,1,0:T(8,128)(2,1)}), bf16[8,128,128]{2,1,0:T(8,128)(2,1)S(1)}, u32[]{:S(2)}, u32[]{:S(2)}) async-start(bf16[8,128,128]{2,1,0:T(8,128)(2,1)} %bitcast), calls=%async_computation | async-start | bytes 524288 | tf_op jit(solution)/shard_map/all_to_all | solution.py:259
  17.0 0.0 collective-permute-done.1.block
  17.1 5.7 %collective-permute-start.2 = (bf16[64,256]{1,0:T(8,128)(2,1)S(1)}, bf16[64,256]{1,0:T(8,128)(2,1)S(1)}, u32[]{:S(2)}, u32[]{:S(2)}) collective-permute-start(bf16[64,256]{1,0:T(8,128)(2,1)S(1)} %forward.1.refs_0_), channel_id=1, source_target_pairs={{0,208},{16,192},{32,240},{48,224},{64,144},{80,128},{96,176},{112... | collective-permute-start | bytes 98312 | tf_op jit(solution)/shard_map/ppermute | solution.py:241
  22.8 0.0 collective-permute-start.3
  22.8 1.1 %collective-permute-start.4 = (bf16[64,256]{1,0:T(8,128)(2,1)S(1)}, bf16[64,256]{1,0:T(8,128)(2,1)S(1)}, u32[]{:S(2)}, u32[]{:S(2)}) collective-permute-start(bf16[64,256]{1,0:T(8,128)(2,1)S(1)} %forward.1.refs_0_), channel_id=1, source_target_pairs={{0,16},{16,0},{32,48},{48,32},{64,80},{80,64},{96,112},{112,96},{1... | collective-permute-start | bytes 98312 | tf_op jit(solution)/shard_map/ppermute | solution.py:241
  23.8 0.8 %collective-permute-done.2.refs_1_ = bf16[64,256]{1,0:T(8,128)(2,1)S(1)} collective-permute-done((bf16[64,256]{1,0:T(8,128)(2,1)S(1)}, bf16[64,256]{1,0:T(8,128)(2,1)S(1)}, u32[]{:S(2)}, u32[]{:S(2)}) %collective-permute-start.2) | collective-permute-done | bytes 32800 | tf_op jit(solution)/shard_map/ppermute | solution.py:241
  24.6 2.1 %collective-permute-done.3.refs_2_ = bf16[64,256]{1,0:T(8,128)(2,1)S(1)} collective-permute-done((bf16[64,256]{1,0:T(8,128)(2,1)S(1)}, bf16[64,256]{1,0:T(8,128)(2,1)S(1)}, u32[]{:S(2)}, u32[]{:S(2)}) %collective-permute-start.3) | collective-permute-done | bytes 32800 | tf_op jit(solution)/shard_map/ppermute | solution.py:241
  26.7 0.0 collective-permute-done.4.refs_3_
  26.7 0.6 %all-to-all-done.parts = bf16[8,128,128]{2,1,0:T(8,128)(2,1)S(1)} async-done(((bf16[8,128,128]{2,1,0:T(8,128)(2,1)}), bf16[8,128,128]{2,1,0:T(8,128)(2,1)S(1)}, u32[]{:S(2)}, u32[]{:S(2)}) %all-to-all-start) | async-done | bytes 262176 | tf_op jit(solution)/shard_map/all_to_all | solution.py:259
  27.4 1.0 %product.1 = (bf16[16,32,128]{2,1,0:T(8,128)(2,1)}, bf16[4,64,256]{2,1,0:T(8,128)(2,1)S(1)}) custom-call(bf16[8,128,128]{2,1,0:T(8,128)(2,1)S(1)} %all-to-all-done.parts, bf16[4,64,256]{2,1,0:T(8,128)(2,1)S(1)} %join.1.queries), custom_call_target="tpu_custom_call" | custom-call | tf_op jit(solution)/shard_map/product/pallas_call | solution.py:154
  28.4 7.9 %all-to-all-start.1 = ((bf16[16,32,128]{2,1,0:T(8,128)(2,1)}), bf16[16,32,128]{2,1,0:T(8,128)(2,1)S(1)}, u32[]{:S(2)}, u32[]{:S(2)}) async-start(bf16[16,32,128]{2,1,0:T(8,128)(2,1)} %get-tuple-element.4), calls=%async_computation.1 | async-start | bytes 262144 | tf_op jit(solution)/shard_map/all_to_all | solution.py:264
  36.3 2.1 %collective-permute-start.5 = (bf16[4,64,256]{2,1,0:T(8,128)(2,1)S(1)}, bf16[4,64,256]{2,1,0:T(8,128)(2,1)S(1)}, u32[]{:S(2)}, u32[]{:S(2)}) collective-permute-start(bf16[4,64,256]{2,1,0:T(8,128)(2,1)S(1)} %get-tuple-element.5.refs_0_), channel_id=1, source_target_pairs={{0,112},{16,96},{32,80},{48,64},{64,48},{80,32},{96,16},{112,0},{1... | collective-permute-start | bytes 393224 | tf_op jit(solution)/shard_map/ppermute | solution.py:241
  38.4 0.7 %collective-permute-start.6 = (bf16[4,64,256]{2,1,0:T(8,128)(2,1)S(1)}, bf16[4,64,256]{2,1,0:T(8,128)(2,1)S(1)}, u32[]{:S(2)}, u32[]{:S(2)}) collective-permute-start(bf16[4,64,256]{2,1,0:T(8,128)(2,1)S(1)} %get-tuple-element.5.refs_0_), channel_id=1, source_target_pairs={{0,64},{16,80},{32,96},{48,112},{64,0},{80,16},{96,32},{112,48},{1... | collective-permute-start | bytes 393224 | tf_op jit(solution)/shard_map/ppermute | solution.py:241
  39.1 1.0 %collective-permute-start.7 = (bf16[4,64,256]{2,1,0:T(8,128)(2,1)S(1)}, bf16[4,64,256]{2,1,0:T(8,128)(2,1)S(1)}, u32[]{:S(2)}, u32[]{:S(2)}) collective-permute-start(bf16[4,64,256]{2,1,0:T(8,128)(2,1)S(1)} %get-tuple-element.5.refs_0_), channel_id=1, source_target_pairs={{0,48},{16,32},{32,16},{48,0},{64,112},{80,96},{96,80},{112,64},{1... | collective-permute-start | bytes 393224 | tf_op jit(solution)/shard_map/ppermute | solution.py:241
  40.1 3.2 %collective-permute-done.5.refs_1_ = bf16[4,64,256]{2,1,0:T(8,128)(2,1)S(1)} collective-permute-done((bf16[4,64,256]{2,1,0:T(8,128)(2,1)S(1)}, bf16[4,64,256]{2,1,0:T(8,128)(2,1)S(1)}, u32[]{:S(2)}, u32[]{:S(2)}) %collective-permute-start.5) | collective-permute-done | bytes 131104 | tf_op jit(solution)/shard_map/ppermute | solution.py:241
  43.3 2.0 %collective-permute-done.6.refs_2_ = bf16[4,64,256]{2,1,0:T(8,128)(2,1)S(1)} collective-permute-done((bf16[4,64,256]{2,1,0:T(8,128)(2,1)S(1)}, bf16[4,64,256]{2,1,0:T(8,128)(2,1)S(1)}, u32[]{:S(2)}, u32[]{:S(2)}) %collective-permute-start.6) | collective-permute-done | bytes 131104 | tf_op jit(solution)/shard_map/ppermute | solution.py:241
  45.4 0.9 %collective-permute-done.7.refs_3_ = bf16[4,64,256]{2,1,0:T(8,128)(2,1)S(1)} collective-permute-done((bf16[4,64,256]{2,1,0:T(8,128)(2,1)S(1)}, bf16[4,64,256]{2,1,0:T(8,128)(2,1)S(1)}, u32[]{:S(2)}, u32[]{:S(2)}) %collective-permute-start.7) | collective-permute-done | bytes 131104 | tf_op jit(solution)/shard_map/ppermute | solution.py:241
  46.2 0.0 all-to-all-done.1.parts
  46.2 0.9 %finish.1 = (bf16[2,256]{1,0:T(2,128)(2,1)}, f32[2,64]{1,0:T(2,128)}) custom-call(bf16[16,32,128]{2,1,0:T(8,128)(2,1)S(1)} %all-to-all-done.1.parts, bf16[4,64,256]{2,1,0:T(8,128)(2,1)S(1)} %get-tuple-element.5.refs_0_, bf16[4,64,256]{2,1,0:T(8,128)(2,1)S(1)} %collective-permute-done.5.refs_1_, bf16[4,64,256]{2,1,0:T(8,128)(2,1)S(1)} %collective-permute-done.6.refs_2_, ...), custom_call_target="tpu_custom_call" | custom-call | tf_op jit(solution)/shard_map/finish/pallas_call | solution.py:209
  (2 shorter events, 0.0 us)
Async XLA Ops:
  0.6 10.6 %copy-start = (bf16[2,1024,1792]{2,1,0:T(8,128)(2,1)S(1)}, bf16[2,1024,1792]{2,1,0:T(8,128)(2,1)}, u32[]{:S(2)}) copy-start(bf16[2,1024,1792]{2,1,0:T(8,128)(2,1)} %acts.3) | copy-start | bytes 22020100
  0.6 10.6 %copy-start.1 = (bf16[2,1024,512]{2,1,0:T(8,128)(2,1)S(1)}, bf16[2,1024,512]{2,1,0:T(8,128)(2,1)}, u32[]{:S(2)}) copy-start(bf16[2,1024,512]{2,1,0:T(8,128)(2,1)} %grads.3) | copy-start | bytes 6291460
  0.7 10.6 %copy-start.2 = (bf16[64,1792]{1,0:T(8,128)(2,1)S(1)}, bf16[64,1792]{1,0:T(8,128)(2,1)}, u32[]{:S(2)}) copy-start(bf16[64,1792]{1,0:T(8,128)(2,1)} %inf.3) | copy-start | bytes 688132
  0.7 10.6 %copy-start.3 = (bf16[64,512]{1,0:T(8,128)(2,1)S(1)}, bf16[64,512]{1,0:T(8,128)(2,1)}, u32[]{:S(2)}) copy-start(bf16[64,512]{1,0:T(8,128)(2,1)} %outf.3) | copy-start | bytes 196612
  0.7 6.9 %copy-start.4 = (bf16[64,256]{1,0:T(8,128)(2,1)S(1)}, bf16[64,256]{1,0:T(8,128)(2,1)}, u32[]{:S(2)}) copy-start(bf16[64,256]{1,0:T(8,128)(2,1)} %param.9) | copy-start | bytes 98308
  4.3 8.4 %collective-permute-start = (f32[1024,128]{1,0:T(8,128)S(1)}, f32[1024,128]{1,0:T(8,128)S(1)}, u32[]{:S(2)}, u32[]{:S(2)}) collective-permute-start(f32[1024,128]{1,0:T(8,128)S(1)} %project.1), channel_id=1, source_target_pairs={{0,1},{1,0},{2,3},{3,2},{4,5},{5,4},{6,7},{7,6},{8,9},{9,8},{10,11... | collective-permute-start | bytes 1572872 | tf_op jit(solution)/shard_map/ppermute | solution.py:245
  7.6 9.4 %collective-permute-start.1 = (bf16[64,256]{1,0:T(8,128)(2,1)S(1)}, bf16[64,256]{1,0:T(8,128)(2,1)S(1)}, u32[]{:S(2)}, u32[]{:S(2)}) collective-permute-start(bf16[64,256]{1,0:T(8,128)(2,1)S(1)} %copy-done.4), channel_id=1, source_target_pairs={{8,0},{9,16},{11,32},{6,48},{7,64},{4,80},{3,96},{5,112},{12,128},... | collective-permute-start | bytes 98312 | tf_op jit(solution)/shard_map/ppermute | solution.py:252
  13.4 14.0 %all-to-all-start = ((bf16[8,128,128]{2,1,0:T(8,128)(2,1)}), bf16[8,128,128]{2,1,0:T(8,128)(2,1)S(1)}, u32[]{:S(2)}, u32[]{:S(2)}) async-start(bf16[8,128,128]{2,1,0:T(8,128)(2,1)} %bitcast), calls=%async_computation | async-start | bytes 524288 | tf_op jit(solution)/shard_map/all_to_all | solution.py:259
  17.1 7.6 %collective-permute-start.2 = (bf16[64,256]{1,0:T(8,128)(2,1)S(1)}, bf16[64,256]{1,0:T(8,128)(2,1)S(1)}, u32[]{:S(2)}, u32[]{:S(2)}) collective-permute-start(bf16[64,256]{1,0:T(8,128)(2,1)S(1)} %forward.1.refs_0_), channel_id=1, source_target_pairs={{0,208},{16,192},{32,240},{48,224},{64,144},{80,128},{96,176},{112... | collective-permute-start | bytes 98312 | tf_op jit(solution)/shard_map/ppermute | solution.py:241
  22.8 4.0 %collective-permute-start.3 = (bf16[64,256]{1,0:T(8,128)(2,1)S(1)}, bf16[64,256]{1,0:T(8,128)(2,1)S(1)}, u32[]{:S(2)}, u32[]{:S(2)}) collective-permute-start(bf16[64,256]{1,0:T(8,128)(2,1)S(1)} %forward.1.refs_0_), channel_id=1, source_target_pairs={{0,192},{16,208},{32,224},{48,240},{64,128},{80,144},{96,160},{112... | collective-permute-start | bytes 98312 | tf_op jit(solution)/shard_map/ppermute | solution.py:241
  22.8 4.0 %collective-permute-start.4 = (bf16[64,256]{1,0:T(8,128)(2,1)S(1)}, bf16[64,256]{1,0:T(8,128)(2,1)S(1)}, u32[]{:S(2)}, u32[]{:S(2)}) collective-permute-start(bf16[64,256]{1,0:T(8,128)(2,1)S(1)} %forward.1.refs_0_), channel_id=1, source_target_pairs={{0,16},{16,0},{32,48},{48,32},{64,80},{80,64},{96,112},{112,96},{1... | collective-permute-start | bytes 98312 | tf_op jit(solution)/shard_map/ppermute | solution.py:241
  28.4 17.9 %all-to-all-start.1 = ((bf16[16,32,128]{2,1,0:T(8,128)(2,1)}), bf16[16,32,128]{2,1,0:T(8,128)(2,1)S(1)}, u32[]{:S(2)}, u32[]{:S(2)}) async-start(bf16[16,32,128]{2,1,0:T(8,128)(2,1)} %get-tuple-element.4), calls=%async_computation.1 | async-start | bytes 262144 | tf_op jit(solution)/shard_map/all_to_all | solution.py:264
  36.3 7.0 %collective-permute-start.5 = (bf16[4,64,256]{2,1,0:T(8,128)(2,1)S(1)}, bf16[4,64,256]{2,1,0:T(8,128)(2,1)S(1)}, u32[]{:S(2)}, u32[]{:S(2)}) collective-permute-start(bf16[4,64,256]{2,1,0:T(8,128)(2,1)S(1)} %get-tuple-element.5.refs_0_), channel_id=1, source_target_pairs={{0,112},{16,96},{32,80},{48,64},{64,48},{80,32},{96,16},{112,0},{1... | collective-permute-start | bytes 393224 | tf_op jit(solution)/shard_map/ppermute | solution.py:241
  38.4 6.9 %collective-permute-start.6 = (bf16[4,64,256]{2,1,0:T(8,128)(2,1)S(1)}, bf16[4,64,256]{2,1,0:T(8,128)(2,1)S(1)}, u32[]{:S(2)}, u32[]{:S(2)}) collective-permute-start(bf16[4,64,256]{2,1,0:T(8,128)(2,1)S(1)} %get-tuple-element.5.refs_0_), channel_id=1, source_target_pairs={{0,64},{16,80},{32,96},{48,112},{64,0},{80,16},{96,32},{112,48},{1... | collective-permute-start | bytes 393224 | tf_op jit(solution)/shard_map/ppermute | solution.py:241
  39.1 7.1 %collective-permute-start.7 = (bf16[4,64,256]{2,1,0:T(8,128)(2,1)S(1)}, bf16[4,64,256]{2,1,0:T(8,128)(2,1)S(1)}, u32[]{:S(2)}, u32[]{:S(2)}) collective-permute-start(bf16[4,64,256]{2,1,0:T(8,128)(2,1)S(1)} %get-tuple-element.5.refs_0_), channel_id=1, source_target_pairs={{0,48},{16,32},{32,16},{48,0},{64,112},{80,96},{96,80},{112,64},{1... | collective-permute-start | bytes 393224 | tf_op jit(solution)/shard_map/ppermute | solution.py:241

commit v5 on v3

--- a/solution.py
+++ b/solution.py
@@ -146,13 +146,11 @@
 
 def product_kernel(parts, queries, out, same, square):
     total = jnp.sum(parts[...].astype(F32), axis=0)
-    square[...] = lax.dot_general(
-        total[:, :RANK],
-        total[:, RANK:],
-        TN,
-        precision=lax.Precision.HIGHEST,
-        preferred_element_type=F32,
-    )
+    high = total.astype(BF16)
+    low = (total - high.astype(F32)).astype(BF16)
+    left = jnp.concatenate([high[:, :RANK], high[:, :RANK], low[:, :RANK]], axis=0)
+    right = jnp.concatenate([high[:, RANK:], low[:, RANK:], high[:, RANK:]], axis=0)
+    square[...] = lax.dot_general(left, right, TN, preferred_element_type=F32)
     half = RANK // 2
     rows = jnp.concatenate(
         [square[pl.ds(0, half, stride=2), :], square[pl.ds(1, half, stride=2), :]], axis=1

time: 47.7 us -> 47.7 us (level)
  no operation moved by 1% of the time
where the time goes in v5:
time: 47.7 us; the launch traced here: 47.2 us
  starting transfers between devices  29.2 us (61%)
  waiting for transfers between devices  9.61 us (20%)
  Pallas kernels  7.66 us (16%)
  between operations  0.71 us (1%)
    ppermute x6, starting transfers between devices, swapped(): return lax.ppermute(x, 'dp', [(i, i ^ bits) for i in range(n_dp)])  10.6 us
    ppermute x6, waiting for transfers between devices, swapped(): return lax.ppermute(x, 'dp', [(i, i ^ bits) for i in range(n_dp)])  9.01 us
    all_to_all x1, starting transfers between devices, local(): everyone = lax.all_to_all(copies, 'tensor', 0, 0)  7.96 us
    ppermute x1, starting transfers between devices, local(): turned = lax.ppermute(block, ('dp', 'tensor'), moves)  3.62 us
    all_to_all x1, starting transfers between devices, local(): lax.all_to_all(pair.reshape(chips, tokens, 2 * RANK), 'tensor', 0, 0, axi...  3.61 us
    pallas_call x1, Pallas kernels, project(): pl.pallas_call(project_kernel, out_shape=(pltpu.VMEM((seq, 2 * RANK), F32...  3.6 us
    ppermute x1, starting transfers between devices, local(): lax.ppermute(sent, 'tensor', [(i, i ^ 1) for i in range(n_tensor)])  3.33 us
    pallas_call x1, Pallas kernels, project_whole(): pl.pallas_call(whole_kernel, out_shape=pltpu.VMEM((seq, 2 * RANK), F32),...  1.43 us
  transfers between devices with their start and end apart: 10, of which 6 were waited for; matrix products, arithmetic and copies ran while one was open for 0% of the time, Pallas kernels for 5%

profile of v5, /device:TPU:1, one launch (start us, length us, event | category | flops | bytes accessed | tf_op | source)
XLA Modules:
  0.0 47.2 jit_solution(6557093344266965167)
XLA Ops:
  0.6 0.0 copy-start
  0.6 0.0 copy-start.1
  0.7 0.0 copy-start.2
  0.7 0.0 copy-start.3
  0.7 3.6 %project.1 = (f32[1024,128]{1,0:T(8,128)S(1)}, bf16[64,256]{1,0:T(8,128)(2,1)S(1)}) custom-call(bf16[2,1024,1792]{2,1,0:T(8,128)(2,1)} %acts.3, bf16[2,1024,512]{2,1,0:T(8,128)(2,1)} %grads.3, bf16[64,1792]{1,0:T(8,128)(2,1)} %inf.3, bf16[64,512]{1,0:T(8,128)(2,1)} %outf.3, bf16[64,256]{1,0:T(8,128)(2,1)} %block.1), custom_call_target="tpu_custom_call" | custom-call | flops 3019898880 | bytes 4718592 | tf_op jit(solution)/shard_map/project/pallas_call | solution.py:45
  4.3 3.3 %collective-permute-start = (f32[1024,128]{1,0:T(8,128)S(1)}, f32[1024,128]{1,0:T(8,128)S(1)}, u32[]{:S(2)}, u32[]{:S(2)}) collective-permute-start(f32[1024,128]{1,0:T(8,128)S(1)} %get-tuple-element.6), channel_id=1, source_target_pairs={{0,1},{1,0},{2,3},{3,2},{4,5},{5,4},{6,7},{7,6},{8,9},{9,8},{10,11... | collective-permute-start | bytes 1572872 | tf_op jit(solution)/shard_map/ppermute | solution.py:255
  7.6 3.6 %collective-permute-start.1 = (bf16[64,256]{1,0:T(8,128)(2,1)S(1)}, bf16[64,256]{1,0:T(8,128)(2,1)S(1)}, u32[]{:S(2)}, u32[]{:S(2)}) collective-permute-start(bf16[64,256]{1,0:T(8,128)(2,1)S(1)} %get-tuple-element.7), channel_id=1, source_target_pairs={{8,0},{9,16},{11,32},{6,48},{7,64},{4,80},{3,96},{5,112},{12,128},... | collective-permute-start | bytes 98312 | tf_op jit(solution)/shard_map/ppermute | solution.py:262
  11.2 0.0 copy-done
  11.2 0.0 copy-done.1
  11.2 0.0 copy-done.2
  11.2 0.0 copy-done.3
  11.2 1.4 %project_whole.1.kept = f32[1024,128]{1,0:T(8,128)S(1)} custom-call(bf16[2,1024,1792]{2,1,0:T(8,128)(2,1)S(1)} %copy-done, bf16[2,1024,512]{2,1,0:T(8,128)(2,1)S(1)} %copy-done.1, bf16[64,1792]{1,0:T(8,128)(2,1)S(1)} %copy-done.2, bf16[64,512]{1,0:T(8,128)(2,1)S(1)} %copy-done.3), custom_call_target="tpu_custom_call" | custom-call | flops 301989888 | bytes 4718592 | tf_op jit(solution)/shard_map/project_whole/pallas_call | solution.py:83
  12.7 0.0 collective-permute-done.arrived
  12.7 0.7 %pair_sum.1.after = bf16[1024,128]{1,0:T(8,128)(2,1)} custom-call(f32[1024,128]{1,0:T(8,128)S(1)} %project_whole.1.kept, f32[1024,128]{1,0:T(8,128)S(1)} %collective-permute-done.arrived), custom_call_target="tpu_custom_call" | custom-call | tf_op jit(solution)/shard_map/pair_sum/pallas_call | solution.py:103
  13.4 3.6 %all-to-all-start = ((bf16[8,128,128]{2,1,0:T(8,128)(2,1)}), bf16[8,128,128]{2,1,0:T(8,128)(2,1)S(1)}, u32[]{:S(2)}, u32[]{:S(2)}) async-start(bf16[8,128,128]{2,1,0:T(8,128)(2,1)} %bitcast), calls=%async_computation | async-start | bytes 524288 | tf_op jit(solution)/shard_map/all_to_all | solution.py:269
  17.0 0.0 collective-permute-done.1.block
  17.0 5.7 %collective-permute-start.2 = (bf16[64,256]{1,0:T(8,128)(2,1)S(1)}, bf16[64,256]{1,0:T(8,128)(2,1)S(1)}, u32[]{:S(2)}, u32[]{:S(2)}) collective-permute-start(bf16[64,256]{1,0:T(8,128)(2,1)S(1)} %forward.1.refs_0_), channel_id=1, source_target_pairs={{0,208},{16,192},{32,240},{48,224},{64,144},{80,128},{96,176},{112... | collective-permute-start | bytes 98312 | tf_op jit(solution)/shard_map/ppermute | solution.py:251
  22.8 0.0 collective-permute-start.3
  22.8 1.0 %collective-permute-start.4 = (bf16[64,256]{1,0:T(8,128)(2,1)S(1)}, bf16[64,256]{1,0:T(8,128)(2,1)S(1)}, u32[]{:S(2)}, u32[]{:S(2)}) collective-permute-start(bf16[64,256]{1,0:T(8,128)(2,1)S(1)} %forward.1.refs_0_), channel_id=1, source_target_pairs={{0,16},{16,0},{32,48},{48,32},{64,80},{80,64},{96,112},{112,96},{1... | collective-permute-start | bytes 98312 | tf_op jit(solution)/shard_map/ppermute | solution.py:251
  23.8 0.8 %collective-permute-done.2.refs_1_ = bf16[64,256]{1,0:T(8,128)(2,1)S(1)} collective-permute-done((bf16[64,256]{1,0:T(8,128)(2,1)S(1)}, bf16[64,256]{1,0:T(8,128)(2,1)S(1)}, u32[]{:S(2)}, u32[]{:S(2)}) %collective-permute-start.2) | collective-permute-done | bytes 32800 | tf_op jit(solution)/shard_map/ppermute | solution.py:251
  24.7 2.1 %collective-permute-done.3.refs_2_ = bf16[64,256]{1,0:T(8,128)(2,1)S(1)} collective-permute-done((bf16[64,256]{1,0:T(8,128)(2,1)S(1)}, bf16[64,256]{1,0:T(8,128)(2,1)S(1)}, u32[]{:S(2)}, u32[]{:S(2)}) %collective-permute-start.3) | collective-permute-done | bytes 32800 | tf_op jit(solution)/shard_map/ppermute | solution.py:251
  26.8 0.0 collective-permute-done.4.refs_3_
  26.8 0.6 %all-to-all-done.parts = bf16[8,128,128]{2,1,0:T(8,128)(2,1)S(1)} async-done(((bf16[8,128,128]{2,1,0:T(8,128)(2,1)}), bf16[8,128,128]{2,1,0:T(8,128)(2,1)S(1)}, u32[]{:S(2)}, u32[]{:S(2)}) %all-to-all-start) | async-done | bytes 262176 | tf_op jit(solution)/shard_map/all_to_all | solution.py:269
  27.4 1.0 %product.1 = (bf16[16,32,128]{2,1,0:T(8,128)(2,1)}, bf16[4,64,256]{2,1,0:T(8,128)(2,1)S(1)}) custom-call(bf16[8,128,128]{2,1,0:T(8,128)(2,1)S(1)} %all-to-all-done.parts, bf16[4,64,256]{2,1,0:T(8,128)(2,1)S(1)} %join.1.queries), custom_call_target="tpu_custom_call" | custom-call | tf_op jit(solution)/shard_map/product/pallas_call | solution.py:164
  28.3 8.0 %all-to-all-start.1 = ((bf16[16,32,128]{2,1,0:T(8,128)(2,1)}), bf16[16,32,128]{2,1,0:T(8,128)(2,1)S(1)}, u32[]{:S(2)}, u32[]{:S(2)}) async-start(bf16[16,32,128]{2,1,0:T(8,128)(2,1)} %get-tuple-element.8), calls=%async_computation.1 | async-start | bytes 262144 | tf_op jit(solution)/shard_map/all_to_all | solution.py:274
  36.3 2.1 %collective-permute-start.5 = (bf16[4,64,256]{2,1,0:T(8,128)(2,1)S(1)}, bf16[4,64,256]{2,1,0:T(8,128)(2,1)S(1)}, u32[]{:S(2)}, u32[]{:S(2)}) collective-permute-start(bf16[4,64,256]{2,1,0:T(8,128)(2,1)S(1)} %get-tuple-element.9.refs_0_), channel_id=1, source_target_pairs={{0,112},{16,96},{32,80},{48,64},{64,48},{80,32},{96,16},{112,0},{1... | collective-permute-start | bytes 393224 | tf_op jit(solution)/shard_map/ppermute | solution.py:251
  38.5 0.7 %collective-permute-start.6 = (bf16[4,64,256]{2,1,0:T(8,128)(2,1)S(1)}, bf16[4,64,256]{2,1,0:T(8,128)(2,1)S(1)}, u32[]{:S(2)}, u32[]{:S(2)}) collective-permute-start(bf16[4,64,256]{2,1,0:T(8,128)(2,1)S(1)} %get-tuple-element.9.refs_0_), channel_id=1, source_target_pairs={{0,64},{16,80},{32,96},{48,112},{64,0},{80,16},{96,32},{112,48},{1... | collective-permute-start | bytes 393224 | tf_op jit(solution)/shard_map/ppermute | solution.py:251
  39.1 1.0 %collective-permute-start.7 = (bf16[4,64,256]{2,1,0:T(8,128)(2,1)S(1)}, bf16[4,64,256]{2,1,0:T(8,128)(2,1)S(1)}, u32[]{:S(2)}, u32[]{:S(2)}) collective-permute-start(bf16[4,64,256]{2,1,0:T(8,128)(2,1)S(1)} %get-tuple-element.9.refs_0_), channel_id=1, source_target_pairs={{0,48},{16,32},{32,16},{48,0},{64,112},{80,96},{96,80},{112,64},{1... | collective-permute-start | bytes 393224 | tf_op jit(solution)/shard_map/ppermute | solution.py:251
  40.2 3.2 %collective-permute-done.5.refs_1_ = bf16[4,64,256]{2,1,0:T(8,128)(2,1)S(1)} collective-permute-done((bf16[4,64,256]{2,1,0:T(8,128)(2,1)S(1)}, bf16[4,64,256]{2,1,0:T(8,128)(2,1)S(1)}, u32[]{:S(2)}, u32[]{:S(2)}) %collective-permute-start.5) | collective-permute-done | bytes 131104 | tf_op jit(solution)/shard_map/ppermute | solution.py:251
  43.3 2.1 %collective-permute-done.6.refs_2_ = bf16[4,64,256]{2,1,0:T(8,128)(2,1)S(1)} collective-permute-done((bf16[4,64,256]{2,1,0:T(8,128)(2,1)S(1)}, bf16[4,64,256]{2,1,0:T(8,128)(2,1)S(1)}, u32[]{:S(2)}, u32[]{:S(2)}) %collective-permute-start.6) | collective-permute-done | bytes 131104 | tf_op jit(solution)/shard_map/ppermute | solution.py:251
  45.4 0.9 %collective-permute-done.7.refs_3_ = bf16[4,64,256]{2,1,0:T(8,128)(2,1)S(1)} collective-permute-done((bf16[4,64,256]{2,1,0:T(8,128)(2,1)S(1)}, bf16[4,64,256]{2,1,0:T(8,128)(2,1)S(1)}, u32[]{:S(2)}, u32[]{:S(2)}) %collective-permute-start.7) | collective-permute-done | bytes 131104 | tf_op jit(solution)/shard_map/ppermute | solution.py:251
  46.3 0.0 all-to-all-done.1.parts
  46.3 0.9 %finish.1 = (bf16[2,256]{1,0:T(2,128)(2,1)}, f32[2,64]{1,0:T(2,128)}) custom-call(bf16[16,32,128]{2,1,0:T(8,128)(2,1)S(1)} %all-to-all-done.1.parts, bf16[4,64,256]{2,1,0:T(8,128)(2,1)S(1)} %get-tuple-element.9.refs_0_, bf16[4,64,256]{2,1,0:T(8,128)(2,1)S(1)} %collective-permute-done.5.refs_1_, bf16[4,64,256]{2,1,0:T(8,128)(2,1)S(1)} %collective-permute-done.6.refs_2_, ...), custom_call_target="tpu_custom_call" | custom-call | tf_op jit(solution)/shard_map/finish/pallas_call | solution.py:219
  (2 shorter events, 0.0 us)
Async XLA Ops:
  0.6 10.6 %copy-start = (bf16[2,1024,1792]{2,1,0:T(8,128)(2,1)S(1)}, bf16[2,1024,1792]{2,1,0:T(8,128)(2,1)}, u32[]{:S(2)}) copy-start(bf16[2,1024,1792]{2,1,0:T(8,128)(2,1)} %acts.3) | copy-start | bytes 22020100
  0.6 10.6 %copy-start.1 = (bf16[2,1024,512]{2,1,0:T(8,128)(2,1)S(1)}, bf16[2,1024,512]{2,1,0:T(8,128)(2,1)}, u32[]{:S(2)}) copy-start(bf16[2,1024,512]{2,1,0:T(8,128)(2,1)} %grads.3) | copy-start | bytes 6291460
  0.7 10.6 %copy-start.2 = (bf16[64,1792]{1,0:T(8,128)(2,1)S(1)}, bf16[64,1792]{1,0:T(8,128)(2,1)}, u32[]{:S(2)}) copy-start(bf16[64,1792]{1,0:T(8,128)(2,1)} %inf.3) | copy-start | bytes 688132
  0.7 10.6 %copy-start.3 = (bf16[64,512]{1,0:T(8,128)(2,1)S(1)}, bf16[64,512]{1,0:T(8,128)(2,1)}, u32[]{:S(2)}) copy-start(bf16[64,512]{1,0:T(8,128)(2,1)} %outf.3) | copy-start | bytes 196612
  4.3 8.4 %collective-permute-start = (f32[1024,128]{1,0:T(8,128)S(1)}, f32[1024,128]{1,0:T(8,128)S(1)}, u32[]{:S(2)}, u32[]{:S(2)}) collective-permute-start(f32[1024,128]{1,0:T(8,128)S(1)} %get-tuple-element.6), channel_id=1, source_target_pairs={{0,1},{1,0},{2,3},{3,2},{4,5},{5,4},{6,7},{7,6},{8,9},{9,8},{10,11... | collective-permute-start | bytes 1572872 | tf_op jit(solution)/shard_map/ppermute | solution.py:255
  7.6 9.4 %collective-permute-start.1 = (bf16[64,256]{1,0:T(8,128)(2,1)S(1)}, bf16[64,256]{1,0:T(8,128)(2,1)S(1)}, u32[]{:S(2)}, u32[]{:S(2)}) collective-permute-start(bf16[64,256]{1,0:T(8,128)(2,1)S(1)} %get-tuple-element.7), channel_id=1, source_target_pairs={{8,0},{9,16},{11,32},{6,48},{7,64},{4,80},{3,96},{5,112},{12,128},... | collective-permute-start | bytes 98312 | tf_op jit(solution)/shard_map/ppermute | solution.py:262
  13.4 13.9 %all-to-all-start = ((bf16[8,128,128]{2,1,0:T(8,128)(2,1)}), bf16[8,128,128]{2,1,0:T(8,128)(2,1)S(1)}, u32[]{:S(2)}, u32[]{:S(2)}) async-start(bf16[8,128,128]{2,1,0:T(8,128)(2,1)} %bitcast), calls=%async_computation | async-start | bytes 524288 | tf_op jit(solution)/shard_map/all_to_all | solution.py:269
  17.0 7.6 %collective-permute-start.2 = (bf16[64,256]{1,0:T(8,128)(2,1)S(1)}, bf16[64,256]{1,0:T(8,128)(2,1)S(1)}, u32[]{:S(2)}, u32[]{:S(2)}) collective-permute-start(bf16[64,256]{1,0:T(8,128)(2,1)S(1)} %forward.1.refs_0_), channel_id=1, source_target_pairs={{0,208},{16,192},{32,240},{48,224},{64,144},{80,128},{96,176},{112... | collective-permute-start | bytes 98312 | tf_op jit(solution)/shard_map/ppermute | solution.py:251
  22.8 4.0 %collective-permute-start.3 = (bf16[64,256]{1,0:T(8,128)(2,1)S(1)}, bf16[64,256]{1,0:T(8,128)(2,1)S(1)}, u32[]{:S(2)}, u32[]{:S(2)}) collective-permute-start(bf16[64,256]{1,0:T(8,128)(2,1)S(1)} %forward.1.refs_0_), channel_id=1, source_target_pairs={{0,192},{16,208},{32,224},{48,240},{64,128},{80,144},{96,160},{112... | collective-permute-start | bytes 98312 | tf_op jit(solution)/shard_map/ppermute | solution.py:251
  22.8 4.0 %collective-permute-start.4 = (bf16[64,256]{1,0:T(8,128)(2,1)S(1)}, bf16[64,256]{1,0:T(8,128)(2,1)S(1)}, u32[]{:S(2)}, u32[]{:S(2)}) collective-permute-start(bf16[64,256]{1,0:T(8,128)(2,1)S(1)} %forward.1.refs_0_), channel_id=1, source_target_pairs={{0,16},{16,0},{32,48},{48,32},{64,80},{80,64},{96,112},{112,96},{1... | collective-permute-start | bytes 98312 | tf_op jit(solution)/shard_map/ppermute | solution.py:251
  28.3 17.9 %all-to-all-start.1 = ((bf16[16,32,128]{2,1,0:T(8,128)(2,1)}), bf16[16,32,128]{2,1,0:T(8,128)(2,1)S(1)}, u32[]{:S(2)}, u32[]{:S(2)}) async-start(bf16[16,32,128]{2,1,0:T(8,128)(2,1)} %get-tuple-element.8), calls=%async_computation.1 | async-start | bytes 262144 | tf_op jit(solution)/shard_map/all_to_all | solution.py:274
  36.3 7.0 %collective-permute-start.5 = (bf16[4,64,256]{2,1,0:T(8,128)(2,1)S(1)}, bf16[4,64,256]{2,1,0:T(8,128)(2,1)S(1)}, u32[]{:S(2)}, u32[]{:S(2)}) collective-permute-start(bf16[4,64,256]{2,1,0:T(8,128)(2,1)S(1)} %get-tuple-element.9.refs_0_), channel_id=1, source_target_pairs={{0,112},{16,96},{32,80},{48,64},{64,48},{80,32},{96,16},{112,0},{1... | collective-permute-start | bytes 393224 | tf_op jit(solution)/shard_map/ppermute | solution.py:251
  38.5 6.9 %collective-permute-start.6 = (bf16[4,64,256]{2,1,0:T(8,128)(2,1)S(1)}, bf16[4,64,256]{2,1,0:T(8,128)(2,1)S(1)}, u32[]{:S(2)}, u32[]{:S(2)}) collective-permute-start(bf16[4,64,256]{2,1,0:T(8,128)(2,1)S(1)} %get-tuple-element.9.refs_0_), channel_id=1, source_target_pairs={{0,64},{16,80},{32,96},{48,112},{64,0},{80,16},{96,32},{112,48},{1... | collective-permute-start | bytes 393224 | tf_op jit(solution)/shard_map/ppermute | solution.py:251
  39.1 7.1 %collective-permute-start.7 = (bf16[4,64,256]{2,1,0:T(8,128)(2,1)S(1)}, bf16[4,64,256]{2,1,0:T(8,128)(2,1)S(1)}, u32[]{:S(2)}, u32[]{:S(2)}) collective-permute-start(bf16[4,64,256]{2,1,0:T(8,128)(2,1)S(1)} %get-tuple-element.9.refs_0_), channel_id=1, source_target_pairs={{0,48},{16,32},{32,16},{48,0},{64,112},{80,96},{96,80},{112,64},{1... | collective-permute-start | bytes 393224 | tf_op jit(solution)/shard_map/ppermute | solution.py:251
